TPU v7x, 768 devices: a whole 4x8x12 slice. The times are simulated.
768 devices in a mesh: dp: 64 (over z_lo, y, core), hid: 12 (over z_hi, x).
Axes of the slice: x: 4, y: 8, z: 12 (z_hi: 3, z_lo: 4; z = z_hi * 4 + z_lo), core: 2. Of those that a mesh axis runs over, the one named last changes fastest.
Arguments:
- tokens: bfloat16 [12288, 4096], P(('dp', 'hid')), may hold values from -6 to 6
- cotangent: bfloat16 [12288, 7680], P('dp', 'hid'), may hold values from -8 to 8
- weights: bfloat16 [2, 7680, 4096], P(None, 'hid'), may hold values from -0.09375 to 0.09375
- basis: bfloat16 [4096, 256], P('dp'), may hold values from -0.09375 to 0.09375
- master: float32 [2, 7680, 4096], P(None, 'hid', 'dp'), may hold values from -0.09375 to 0.09375
- first_moment: float32 [7680, 2, 256], P(('hid', 'dp')), may hold values from -48 to 48
- second_moment: float32 [7680, 2, 256], P(('hid', 'dp')), may hold values from 25 to 2500
Outputs:
- master_new: float32 [2, 7680, 4096], P(None, 'hid', 'dp')
- first_new: float32 [7680, 2, 256], P(('hid', 'dp'))
- second_new: float32 [7680, 2, 256], P(('hid', 'dp'))
All inputs are finite; a program needn't handle non-finite values.
Results may differ from a plain program's by a relative error of at most 0.0003.
Values may be sent and summed in bfloat16 or wider, within the bound.
A program may use at most 64 MiB of HBM per device.

v0:
```python
import jax
import jax.numpy as jnp
from jax import lax
from jax.sharding import PartitionSpec as P

beta_first = 0.9
beta_second = 0.95
step_size = 0.05
adam_epsilon = 1e-08


def silu_pieces(pre_gate):
    sigmoid_val = jax.nn.sigmoid(pre_gate)
    return (pre_gate * sigmoid_val, sigmoid_val * (1.0 + pre_gate * (1.0 - sigmoid_val)))


def on_device(tokens, cotangent, weights, basis, master, first_moment, second_moment):
    highest = lax.Precision.HIGHEST
    group_tokens = lax.all_gather(tokens, "hid", axis=0, tiled=True)
    projected = jnp.dot(
        group_tokens,
        lax.all_gather(basis, "dp", axis=0, tiled=True),
        preferred_element_type=jnp.float32,
    )
    contract_cols = (((1,), (1,)), ((), ()))
    pre_gate = lax.dot_general(
        group_tokens, weights[0], contract_cols, preferred_element_type=jnp.float32
    )
    pre_up = lax.dot_general(
        group_tokens, weights[1], contract_cols, preferred_element_type=jnp.float32
    )
    activated, silu_slope = silu_pieces(pre_gate)
    upstream = cotangent.astype(jnp.float32)
    grad_gate = upstream * pre_up * silu_slope
    grad_up = upstream * activated
    over_tokens = (((0,), (0,)), ((), ()))
    gate_term = lax.dot_general(
        grad_gate, projected, over_tokens, precision=highest, preferred_element_type=jnp.float32
    )
    up_term = lax.dot_general(
        grad_up, projected, over_tokens, precision=highest, preferred_element_type=jnp.float32
    )
    gradient = lax.psum_scatter(
        jnp.stack([gate_term, up_term], axis=1), "dp", scatter_dimension=0, tiled=True
    )
    first_new = beta_first * first_moment + (1.0 - beta_first) * gradient
    second_new = beta_second * second_moment + (1.0 - beta_second) * gradient * gradient
    direction_share = first_new / (jnp.sqrt(second_new) + adam_epsilon)
    direction = lax.all_gather(direction_share, "dp", axis=0, tiled=True)
    lifted = jnp.einsum("fwr,dr->wfd", direction, basis.astype(jnp.float32), precision=highest)
    master_new = master - step_size * lifted
    return (master_new, first_new, second_new)


def solution(mesh):
    in_specs = (
        P(("dp", "hid"), None),
        P("dp", "hid"),
        P(None, "hid", None),
        P("dp", None),
        P(None, "hid", "dp"),
        P(("hid", "dp"), None, None),
        P(("hid", "dp"), None, None),
    )
    out_specs = (P(None, "hid", "dp"), P(("hid", "dp"), None, None), P(("hid", "dp"), None, None))
    return jax.shard_map(
        on_device, mesh=mesh, in_specs=in_specs, out_specs=out_specs, check_vma=False
    )
```

profile of v0, /device:TPU:1, one launch (start us, length us, event | category | flops | bytes accessed | tf_op | source)
XLA Modules:
  0.0 887.7 jit_solution(12532267609257077316)
XLA Ops:
  7.2 0.0 all-gather.4.cloned.1.call-start
  7.2 0.7 all-gather.4.cloned.1.call-update
  7.9 0.0 all-gather.6.cloned.1.call-start
  7.9 0.7 all-gather.6.cloned.1.call-update
  8.6 0.0 copy-start.5
  8.7 0.0 all-reduce.3.cloned.1.call-start
  8.7 94.6 %all-gather.4.cloned.1.call-done = bf16[192,4096]{1,0:T(8,128)(2,1)} async-done(((bf16[16,4096]{1,0:T(8,128)(2,1)}), bf16[192,4096]{1,0:T(8,128)(2,1)}) %all-gather.4.cloned.1.call-update) | async-done | bytes 1572880 | tf_op jit(solution)/shard_map/all_gather | solution.py:19
  103.3 0.0 copy-start
  103.3 4.9 fusion
  108.2 0.0 copy-done.5
  108.2 0.0 copy-done
  108.2 4.4 fusion.11
  112.6 110.9 %all-gather.6.cloned.1.call-done = bf16[4096,256]{1,0:T(8,128)(2,1)} async-done(((bf16[64,256]{1,0:T(8,128)(2,1)}), bf16[4096,256]{1,0:T(8,128)(2,1)}) %all-gather.6.cloned.1.call-update) | async-done | bytes 2097168 | tf_op jit(solution)/shard_map/all_gather | solution.py:22
  223.5 2.2 fusion.29
  225.7 1.3 convolution_bitcast_fusion
  227.0 1.3 convolution_bitcast_fusion.1
  228.3 0.1 pad_maximum_fusion
  228.4 0.0 copy-start.3
  228.4 0.0 copy-start.4
  228.4 0.0 copy-start.1
  228.4 0.0 copy-start.2
  228.4 2.1 copy.14
  230.5 0.0 all-reduce.3.cloned.1.call-update
  230.6 0.0 all-gather.8.cloned.1.call-start
  230.6 1.3 dynamic-slice
  232.5 526.0 %all-reduce.3.cloned.1.call-done = f32[640,2,256]{2,1,0:T(2,128)} async-done(((f32[640,2,256]{2,1,0:T(2,128)}), f32[640,2,256]{2,1,0:T(2,128)}) %all-reduce.3.cloned.1.call-update) | async-done | bytes 1310736
  758.6 0.0 copy-done.3
  758.6 0.0 copy-done.4
  758.6 1.4 add_divide_fusion.2
  760.0 0.0 all-gather.8.cloned.1.call-update
  760.0 118.4 %all-gather.8.cloned.1.call-done = f32[640,2,256]{2,1,0:T(2,128)} async-done(((f32[10,2,256]{2,1,0:T(2,128)}), f32[640,2,256]{2,1,0:T(2,128)}) %all-gather.8.cloned.1.call-update) | async-done | bytes 1310736 | tf_op jit(solution)/shard_map/all_gather | solution.py:49
  878.3 0.0 copy-done.1
  878.3 0.0 copy-done.2
  878.3 2.8 fusion.20
Async XLA Ops:
  7.2 96.1 %all-gather.4.cloned.1.call-start = ((), (), s32[]{:S(2)}) async-start(), calls=%async_computation | async-start | bytes 1703936 | tf_op jit(solution)/shard_map/all_gather | solution.py:19
  7.9 215.6 %all-gather.6.cloned.1.call-start = ((), (), s32[]{:S(2)}) async-start(), calls=%async_computation.1 | async-start | bytes 2129920 | tf_op jit(solution)/shard_map/all_gather | solution.py:22
  8.6 99.6 %copy-start.5 = (bf16[192,640]{1,0:T(8,128)(2,1)S(1)}, bf16[192,640]{1,0:T(8,128)(2,1)}, u32[]{:S(2)}) copy-start(bf16[192,640]{1,0:T(8,128)(2,1)} %param.8) | copy-start | bytes 737284
  8.7 749.9 %all-reduce.3.cloned.1.call-start = ((), (), s32[]{:S(2)}) async-start(), calls=%async_computation.3 | async-start | bytes 2621440
  103.3 5.0 copy-start
  228.4 530.2 %copy-start.3 = (f32[10,2,256]{2,1,0:T(2,128)S(1)}, f32[10,2,256]{2,1,0:T(2,128)}, u32[]{:S(2)}) copy-start(f32[10,2,256]{2,1,0:T(2,128)} %param.13) | copy-start | bytes 61444
  228.4 530.2 %copy-start.4 = (f32[10,2,256]{2,1,0:T(2,128)S(1)}, f32[10,2,256]{2,1,0:T(2,128)}, u32[]{:S(2)}) copy-start(f32[10,2,256]{2,1,0:T(2,128)} %param.12) | copy-start | bytes 61444
  228.4 649.9 %copy-start.1 = (f32[2,640,64]{1,2,0:T(8,128)S(1)}, f32[2,640,64]{1,2,0:T(8,128)}, u32[]{:S(2)}) copy-start(f32[2,640,64]{1,2,0:T(8,128)} %param.11) | copy-start | bytes 983044
  228.4 649.9 %copy-start.2 = (bf16[64,256]{1,0:T(8,128)(2,1)S(1)}, bf16[64,256]{1,0:T(8,128)(2,1)}, u32[]{:S(2)}) copy-start(bf16[64,256]{1,0:T(8,128)(2,1)} %param.10) | copy-start | bytes 98308
  230.6 647.8 %all-gather.8.cloned.1.call-start = ((), (), s32[]{:S(2)}) async-start(), calls=%async_computation.2 | async-start | bytes 1331200 | tf_op jit(solution)/shard_map/all_gather | solution.py:49
Sparse Core Ops, SparseCore 0:
  12.0 91.2 all-gather.3
  105.7 117.7 all-gather.5
  230.7 527.8 all-reduce.2
  761.7 116.5 all-gather.7
where the time goes:
time: 888 us
  waiting for transfers between devices  851 us (96%)
  matrix products  16.9 us (2%)
  between operations  14.5 us (2%)
    unnamed x5, waiting for transfers between devices  527 us
    all_gather x1, waiting for transfers between devices, on_device(): direction = lax.all_gather(direction_share, 'dp', axis=0, tiled=True)  118 us
    all_gather x1, waiting for transfers between devices, on_device(): lax.all_gather(basis, 'dp', axis=0, tiled=True)  111 us
    all_gather x1, waiting for transfers between devices, on_device(): group_tokens = lax.all_gather(tokens, 'hid', axis=0, tiled=True)  94.6 us
  transfers between devices with their start and end apart: 4, of which 4 were waited for; matrix products, arithmetic and copies ran while one was open for 1% of the time, Pallas kernels for 0%

commit v1 on v0

v1 whole, which is shorter than its diff:
```python
import functools

import jax
import jax.numpy as jnp
from jax import lax
from jax.experimental import pallas as pl
from jax.experimental.pallas import tpu as pltpu
from jax.sharding import PartitionSpec as P

MESH = pl.DeviceIdType.MESH
F32 = jnp.float32
BF16 = jnp.bfloat16

beta_first = 0.9
beta_second = 0.95
step_size = 0.05
adam_epsilon = 1e-08

NX, NY, NL, NH = 4, 8, 4, 3
D, HID, RANK, TOK = 4096, 640, 256, 16
GROUP = 192
CHUNKS = 4
CW = D // CHUNKS
HALF = RANK // 2
SHARE = 10
BLOCK = 4 * SHARE
NB = NY * NL


def dot_nt(a, b):
    return lax.dot_general(a, b, (((1,), (1,)), ((), ())), preferred_element_type=F32)


def dot_nn(a, b):
    return lax.dot_general(a, b, (((1,), (0,)), ((), ())), preferred_element_type=F32)


def split(a):
    hi = a.astype(BF16)
    return hi, (a - hi.astype(F32)).astype(BF16)


def kernel(
    tok_in, cot_in, w_in, bas_in, mas_in, fm_in, sm_in,
    mas_out, fn_out, sn_out,
    tok, w, bas, cot, mas, fm, sm, fmx, smx, fmb, smb,
    cot_t, pre, grad, halves, swap, total, part_a, part_b, mid_a, mid_b, last_a, last_b,
    dirs, dirs_w, fn_b, sn_b, fn_x, sn_x,
    local_sem, z_send, z_recv, x_send, x_recv, xx_send, xx_recv,
    bz_send, bz_recv, by_send, by_recv, bf_send, bf_recv, bc_send, bc_recv,
    m_send, m_recv, s_send, s_recv, r1_send, r1_recv, r2_send, r2_recv,
    g1_send, g1_recv, g2_send, g2_recv, gc_send, gc_recv, o_send, o_recv,
):
    dp, hid = lax.axis_index("dp"), lax.axis_index("hid")
    core = lax.rem(dp, 2)
    y = lax.rem(lax.div(dp, 2), NY)
    zl = lax.div(dp, 2 * NY)
    x = lax.rem(hid, NX)
    zh = lax.div(hid, NX)

    def at(core_=core, y_=y, zl_=zl, x_=x, zh_=zh):
        return {"dp": (zl_ * NY + y_) * 2 + core_, "hid": zh_ * NX + x_}

    def turn(v, by, n):
        return lax.rem(v + (by + n), n)

    x_up, x_down = turn(x, 1, NX), turn(x, -1, NX)
    y_up, y_down = turn(y, 1, NY), turn(y, -1, NY)
    mate = at(core_=1 - core)

    peers = [at(x_=x_up), at(x_=x_down), mate]
    peers += [at(zh_=turn(zh, o, NH)) for o in range(1, NH)]
    peers += [at(zl_=turn(zl, o, NL)) for o in range(1, NL)]
    peers += [at(y_=turn(y, o, NY)) for o in range(1, NY)]

    loads = [
        pltpu.make_async_copy(tok_in, tok.at[pl.ds(pl.multiple_of(hid * TOK, TOK), TOK)], local_sem.at[0]),
        pltpu.make_async_copy(bas_in, bas.at[dp], local_sem.at[1]),
        pltpu.make_async_copy(fm_in, fm, local_sem.at[2]),
        pltpu.make_async_copy(sm_in, sm, local_sem.at[3]),
        pltpu.make_async_copy(cot_in, cot, local_sem.at[4]),
        pltpu.make_async_copy(w_in, w, local_sem.at[5]),
        pltpu.make_async_copy(mas_in, mas, local_sem.at[6]),
    ]
    for load in loads:
        load.start()

    barrier = pltpu.get_barrier_semaphore()
    for peer in peers:
        pl.semaphore_signal(barrier, inc=1, device_id=peer, device_id_type=MESH)
    pl.semaphore_wait(barrier, len(peers))

    sends = []

    def remote(src, dst, send, recv, to):
        return pltpu.make_async_remote_copy(
            src_ref=src, dst_ref=dst, send_sem=send, recv_sem=recv, device_id=to, device_id_type=MESH
        )

    def push(*args):
        copy = remote(*args)
        copy.start()
        sends.append(copy)

    def rows_of(zh_, x_):
        return pl.ds(pl.multiple_of((zh_ * NX + x_) * TOK, TOK), TOK)

    def columns(k, half=None):
        if half is None:
            return pl.ds(k * CW, CW)
        return pl.ds(k * CW + half * (CW // 2), CW // 2)

    own_rows = rows_of(zh, x)

    def z_copy(o, k, source_zh, to):
        spot = tok.at[rows_of(source_zh, x), columns(k)]
        src = tok_in.at[:, columns(k)] if o is None else spot
        return src, spot, to

    def send_z(k):
        for o in (1, 2):
            push(tok_in.at[:, columns(k)], tok.at[own_rows, columns(k)], z_send.at[o - 1, k], z_recv.at[o - 1, k],
                 at(zh_=turn(zh, o, NH)))

    def wait_z(k):
        for o in (1, 2):
            spot = tok.at[rows_of(turn(zh, -o, NH), x), columns(k)]
            remote(spot, spot, z_send.at[o - 1, k], z_recv.at[o - 1, k], at(zh_=turn(zh, -o, NH))).wait_recv()

    def send_x(h, k):
        rows = rows_of(turn(zh, -h, NH), x)
        src = tok_in.at[:, columns(k)] if h == 0 else tok.at[rows, columns(k)]
        for d, to in enumerate((x_up, x_down)):
            push(src, tok.at[rows, columns(k)], x_send.at[h, d, k], x_recv.at[h, d, k], at(x_=to))

    def pass_x(h, k):
        source = turn(zh, -h, NH)
        for d, (came, to) in enumerate(((x_down, x_up), (x_up, x_down))):
            spot = tok.at[rows_of(source, came), columns(k)]
            remote(spot, spot, x_send.at[h, d, k], x_recv.at[h, d, k], at(x_=came)).wait_recv()
            piece = tok.at[rows_of(source, came), columns(k, d)]
            push(piece, piece, xx_send.at[h, d, k], xx_recv.at[h, d, k], at(x_=to))

    def wait_xx(k):
        for h in range(NH):
            rows = rows_of(turn(zh, -h, NH), turn(x, 2, NX))
            for d in range(2):
                piece = tok.at[rows, columns(k, d)]
                remote(piece, piece, xx_send.at[h, d, k], xx_recv.at[h, d, k], at(x_=x_up)).wait_recv()

    def shard(zl_, y_, core_=core):
        return bas.at[(zl_ * NY + y_) * 2 + core_]

    def send_bz():
        for o in range(1, NL):
            push(bas_in, shard(zl, y), bz_send.at[o - 1], bz_recv.at[o - 1], at(zl_=turn(zl, o, NL)))

    def send_y(o, step):
        source = turn(zl, -o, NL)
        for d, to in enumerate((y_up, y_down)):
            sign = -1 if d == 0 else 1
            spot = shard(source, turn(y, sign * step, NY))
            if step == 3:
                spot = spot.at[pl.ds(32 * d, 32)]
                push(spot, spot, bf_send.at[o, d], bf_recv.at[o, d], at(y_=to))
            else:
                src = bas_in if o == 0 and step == 0 else spot
                push(src, spot, by_send.at[o, d, step], by_recv.at[o, d, step], at(y_=to))

    def wait_y(o, step):
        source = turn(zl, -o, NL)
        for d, came in enumerate((y_down, y_up)):
            sign = -1 if d == 0 else 1
            spot = shard(source, turn(y, sign * (step + 1), NY))
            if step == 3:
                spot = spot.at[pl.ds(32 * d, 32)]
                remote(spot, spot, bf_send.at[o, d], bf_recv.at[o, d], at(y_=came)).wait_recv()
            else:
                remote(spot, spot, by_send.at[o, d, step], by_recv.at[o, d, step], at(y_=came)).wait_recv()

    def wait_bz(o):
        spot = shard(turn(zl, -o, NL), y)
        remote(spot, spot, bz_send.at[o - 1], bz_recv.at[o - 1], at(zl_=turn(zl, -o, NL))).wait_recv()

    def send_bc(o, r):
        spot = shard(turn(zl, -o, NL), turn(y, r, NY))
        push(spot, spot, bc_send.at[o, r], bc_recv.at[o, r], mate)

    def wait_bc(o, r):
        spot = shard(turn(zl, -o, NL), turn(y, r, NY), 1 - core)
        remote(spot, spot, bc_send.at[o, r], bc_recv.at[o, r], mate).wait_recv()

    push(fm_in, fmx, m_send.at[0], m_recv.at[0], mate)
    push(sm_in, smx, m_send.at[1], m_recv.at[1], mate)
    send_bz()
    send_y(0, 0)
    for k in range(CHUNKS):
        send_z(k)
        send_x(0, k)
    loads[1].wait()
    send_bc(0, 0)

    loads[4].wait()
    cot_t[...] = cot[...].astype(F32).T

    for o in range(1, NL):
        wait_bz(o)
        send_y(o, 0)
        send_bc(o, 0)

    loads[0].wait()
    loads[5].wait()

    def products(k):
        def body(i, carry):
            rows = pl.ds(pl.multiple_of(i * HID, HID), HID)
            term = dot_nt(w[rows, columns(k)], tok[:, columns(k)])
            if k == 0:
                pre[rows, :] = term
            else:
                pre[rows, :] += term
            return carry

        lax.fori_loop(0, 2, body, 0)

    for k in range(CHUNKS):
        wait_z(k)
        send_x(1, k)
        send_x(2, k)
        pass_x(0, k)
        if k >= 1:
            pass_x(1, k - 1)
            pass_x(2, k - 1)
        for o in range(NL):
            wait_y(o, k)
            if k < 3:
                send_y(o, k + 1)
                for r in (-(k + 1), k + 1):
                    send_bc(o, r % NY)
            else:
                send_bc(o, 4)
        if k >= 2:
            wait_xx(k - 2)
            products(k - 2)
    pass_x(1, CHUNKS - 1)
    pass_x(2, CHUNKS - 1)

    loads[2].wait()
    loads[3].wait()
    for i, spot in enumerate((fmx, smx)):
        remote(spot, spot, m_send.at[i], m_recv.at[i], mate).wait_recv()
    first = core == 0
    for own, other, block in ((fm, fmx, fmb), (sm, smx, smb)):
        for g in range(2):
            mine, theirs = own[:, g, :], other[:, g, :]
            low = jnp.where(first, mine, theirs)
            high = jnp.where(first, theirs, mine)
            base = g * 2 * SHARE
            block[pl.ds(base, SHARE), :] = jnp.where(first, low[:, :HALF], low[:, HALF:])
            block[pl.ds(base + SHARE, SHARE), :] = jnp.where(first, high[:, :HALF], high[:, HALF:])

    wait_xx(CHUNKS - 2)
    products(CHUNKS - 2)
    for o in range(NL):
        for r in range(NY):
            wait_bc(o, r)
    wait_xx(CHUNKS - 1)
    products(CHUNKS - 1)

    projected = dot_nn(tok[...], bas[...].reshape(D, RANK))
    proj_hi, proj_lo = split(projected)

    def backward(i, carry):
        rows = pl.ds(pl.multiple_of(i * 320, 320), 320)
        up_rows = pl.ds(pl.multiple_of(HID + i * 320, 320), 320)
        pre_gate, pre_up, upstream = pre[rows, :], pre[up_rows, :], cot_t[rows, :]
        s = jax.nn.sigmoid(pre_gate)
        grad_gate = upstream * pre_up * (s * (1.0 + pre_gate * (1.0 - s)))
        grad_up = upstream * (pre_gate * s)
        for g, value in enumerate((grad_gate, grad_up)):
            hi, lo = split(value)
            grad[g, rows, :] = dot_nn(hi, proj_hi) + dot_nn(lo, proj_hi) + dot_nn(hi, proj_lo)
        return carry

    lax.fori_loop(0, 2, backward, 0)

    def to_blocks(m, carry):
        rows = pl.ds(pl.multiple_of(m * BLOCK, BLOCK), BLOCK)
        gate, up = grad[0, rows, :], grad[1, rows, :]
        n = 2 * SHARE
        for j in range(2):
            for h in range(2):
                lanes = slice(h * HALF, (h + 1) * HALF)
                halves[h, 2 * m + j, pl.ds(0, n), :] = gate[j * n:(j + 1) * n, lanes]
                halves[h, 2 * m + j, pl.ds(n, n), :] = up[j * n:(j + 1) * n, lanes]
        return carry

    lax.fori_loop(0, NB // 2, to_blocks, 0)

    push(halves.at[1 - core], swap, s_send, s_recv, mate)
    remote(swap, swap, s_send, s_recv, mate).wait_recv()

    def add_swap(b, carry):
        total[lax.div(b, NY), lax.rem(b, NY)] = halves[core, b] + swap[b]
        return carry

    lax.fori_loop(0, NB, add_swap, 0)

    def adam(g):
        first_new = beta_first * fmb[...] + (1.0 - beta_first) * g
        second_new = beta_second * smb[...] + (1.0 - beta_second) * g * g
        fn_b[...] = first_new
        sn_b[...] = second_new
        dirs[core, zl, y] = first_new / (jnp.sqrt(second_new) + adam_epsilon)

    def swap_outputs():
        for i, (src, dst) in enumerate(((fn_b, fn_x), (sn_b, sn_x))):
            remote(src, dst, o_send.at[i], o_recv.at[i], mate).start()

    block = dirs.at[core, zl, y]
    @pl.when(core == 0)
    def _():
        copies = []

        def go(*args):
            copy = remote(*args)
            copy.start()
            copies.append(copy)

        for o in range(1, NY):
            go(total.at[:, turn(y, o, NY)], part_a.at[o - 1], r1_send.at[o - 1], r1_recv.at[o - 1], at(y_=turn(y, o, NY)))
        value = total[:, y]
        for o in range(1, NY):
            remote(part_a.at[o - 1], part_a.at[o - 1], r1_send.at[o - 1], r1_recv.at[o - 1], at(y_=turn(y, -o, NY))).wait_recv()
            value += part_a[o - 1]
        mid_a[...] = value
        for o in range(1, NL):
            go(mid_a.at[turn(zl, o, NL)], last_a.at[o - 1], r2_send.at[o - 1], r2_recv.at[o - 1], at(zl_=turn(zl, o, NL)))
        value = mid_a[zl]
        for o in range(1, NL):
            remote(last_a.at[o - 1], last_a.at[o - 1], r2_send.at[o - 1], r2_recv.at[o - 1], at(zl_=turn(zl, -o, NL))).wait_recv()
            value += last_a[o - 1]
        adam(value)
        for o in range(1, NL):
            go(block, block, g1_send.at[o - 1], g1_recv.at[o - 1], at(zl_=turn(zl, o, NL)))
        swap_outputs()
        for o in range(1, NL):
            spot = dirs.at[core, turn(zl, -o, NL), y]
            remote(spot, spot, g1_send.at[o - 1], g1_recv.at[o - 1], at(zl_=turn(zl, -o, NL))).wait_recv()
        column = dirs.at[core, :, y]
        for o in range(1, NY):
            go(column, column, g2_send.at[o - 1], g2_recv.at[o - 1], at(y_=turn(y, o, NY)))
        go(column, column, gc_send.at[0], gc_recv.at[0], mate)
        for o in range(1, NY):
            spot = dirs.at[core, :, turn(y, -o, NY)]
            remote(spot, spot, g2_send.at[o - 1], g2_recv.at[o - 1], at(y_=turn(y, -o, NY))).wait_recv()
            go(spot, spot, gc_send.at[o], gc_recv.at[o], mate)
        for o in range(NL):
            spot = dirs.at[1 - core, turn(zl, -o, NL)]
            remote(spot, spot, gc_send.at[NY + o], gc_recv.at[NY + o], mate).wait_recv()
        for copy in copies:
            copy.wait_send()

    @pl.when(core == 1)
    def _():
        copies = []

        def go(*args):
            copy = remote(*args)
            copy.start()
            copies.append(copy)

        for o in range(1, NL):
            go(total.at[turn(zl, o, NL)], part_b.at[o - 1], r1_send.at[o - 1], r1_recv.at[o - 1], at(zl_=turn(zl, o, NL)))
        value = total[zl]
        for o in range(1, NL):
            remote(part_b.at[o - 1], part_b.at[o - 1], r1_send.at[o - 1], r1_recv.at[o - 1], at(zl_=turn(zl, -o, NL))).wait_recv()
            value += part_b[o - 1]
        mid_b[...] = value
        for o in range(1, NY):
            go(mid_b.at[turn(y, o, NY)], last_b.at[o - 1], r2_send.at[o - 1], r2_recv.at[o - 1], at(y_=turn(y, o, NY)))
        value = mid_b[y]
        for o in range(1, NY):
            remote(last_b.at[o - 1], last_b.at[o - 1], r2_send.at[o - 1], r2_recv.at[o - 1], at(y_=turn(y, -o, NY))).wait_recv()
            value += last_b[o - 1]
        adam(value)
        for o in range(1, NY):
            go(block, block, g1_send.at[o - 1], g1_recv.at[o - 1], at(y_=turn(y, o, NY)))
        swap_outputs()
        for o in range(1, NY):
            spot = dirs.at[core, zl, turn(y, -o, NY)]
            remote(spot, spot, g1_send.at[o - 1], g1_recv.at[o - 1], at(y_=turn(y, -o, NY))).wait_recv()
        row = dirs.at[core, zl]
        for o in range(1, NL):
            go(row, row, g2_send.at[o - 1], g2_recv.at[o - 1], at(zl_=turn(zl, o, NL)))
        go(row, row, gc_send.at[NY], gc_recv.at[NY], mate)
        for o in range(1, NL):
            spot = dirs.at[core, turn(zl, -o, NL)]
            remote(spot, spot, g2_send.at[o - 1], g2_recv.at[o - 1], at(zl_=turn(zl, -o, NL))).wait_recv()
            go(spot, spot, gc_send.at[NY + o], gc_recv.at[NY + o], mate)
        for o in range(NY):
            spot = dirs.at[1 - core, :, turn(y, -o, NY)]
            remote(spot, spot, gc_send.at[o], gc_recv.at[o], mate).wait_recv()
        for copy in copies:
            copy.wait_send()

    for i, (own, other, out) in enumerate(((fn_b, fn_x, fn_out), (sn_b, sn_x, sn_out))):
        copy = remote(own, other, o_send.at[i], o_recv.at[i], mate)
        copy.wait_recv()
        for g in range(2):
            base = g * 2 * SHARE
            mine = jnp.where(first, own[pl.ds(base, SHARE), :], own[pl.ds(base + SHARE, SHARE), :])
            theirs = jnp.where(first, other[pl.ds(base, SHARE), :], other[pl.ds(base + SHARE, SHARE), :])
            out[:, g, pl.ds(0, HALF)] = jnp.where(first, mine, theirs)
            out[:, g, pl.ds(HALF, HALF)] = jnp.where(first, theirs, mine)
        copy.wait_send()

    def from_blocks(m, carry):
        rows = pl.ds(pl.multiple_of(m * BLOCK, BLOCK), BLOCK)
        n = 2 * SHARE
        for h in range(2):
            lanes = pl.ds(h * HALF, HALF)
            even = dirs[h, lax.div(m, NY // 2), 2 * lax.rem(m, NY // 2)]
            odd = dirs[h, lax.div(m, NY // 2), 2 * lax.rem(m, NY // 2) + 1]
            dirs_w[0, rows, lanes] = jnp.concatenate([even[:n], odd[:n]], axis=0)
            dirs_w[1, rows, lanes] = jnp.concatenate([even[n:], odd[n:]], axis=0)
        return carry

    lax.fori_loop(0, NB // 2, from_blocks, 0)

    loads[6].wait()
    basis_own = bas[dp]
    for g in range(2):
        hi, lo = split(dirs_w[g])
        lifted = dot_nt(basis_own, hi) + dot_nt(basis_own, lo)
        mas_out[g] = mas[g] - step_size * lifted

    for copy in sends:
        copy.wait_send()


def on_device(tokens, cotangent, weights, basis, master, first_moment, second_moment):
    dma, vmem = pltpu.SemaphoreType.DMA, pltpu.VMEM
    share = (SHARE, 2, RANK)
    scratch = [
        vmem((GROUP, D), BF16), vmem((2 * HID, D), BF16), vmem((2 * NB, 64, RANK), BF16), vmem((GROUP, HID), BF16),
        vmem((2, 64, HID), F32), vmem(share, F32), vmem(share, F32), vmem(share, F32), vmem(share, F32),
        vmem((BLOCK, HALF), F32), vmem((BLOCK, HALF), F32),
        vmem((HID, GROUP), F32), vmem((2 * HID, GROUP), F32), vmem((2, HID, RANK), F32),
        vmem((2, NB, BLOCK, HALF), F32), vmem((NB, BLOCK, HALF), F32), vmem((NL, NY, BLOCK, HALF), F32),
        vmem((NY - 1, NL, BLOCK, HALF), F32), vmem((NL - 1, NY, BLOCK, HALF), F32),
        vmem((NL, BLOCK, HALF), F32), vmem((NY, BLOCK, HALF), F32),
        vmem((NL - 1, BLOCK, HALF), F32), vmem((NY - 1, BLOCK, HALF), F32),
        vmem((2, NL, NY, BLOCK, HALF), F32), vmem((2, HID, RANK), F32),
        vmem((BLOCK, HALF), F32), vmem((BLOCK, HALF), F32), vmem((BLOCK, HALF), F32), vmem((BLOCK, HALF), F32),
        dma((7,)),
    ]
    for shape in (
        (2, CHUNKS), (NH, 2, CHUNKS), (NH, 2, CHUNKS), (NL - 1,), (NL, 2, 3), (NL, 2), (NL, NY),
        (2,), None, (NY - 1,), (NY - 1,), (NY - 1,), (NY - 1,), (NY + NL,), (2,),
    ):
        scratch += [dma if shape is None else dma(shape)] * 2
    any_space = pl.BlockSpec(memory_space=pl.ANY)
    in_vmem = pl.BlockSpec(memory_space=pltpu.VMEM)
    master_new, first_new, second_new = pl.pallas_call(
        kernel,
        out_shape=(
            jax.ShapeDtypeStruct((2, 64, HID), F32),
            jax.ShapeDtypeStruct(share, F32),
            jax.ShapeDtypeStruct(share, F32),
        ),
        in_specs=[any_space] * 7,
        out_specs=(in_vmem,) * 3,
        scratch_shapes=scratch,
        compiler_params=pltpu.CompilerParams(
            collective_id=0, has_side_effects=True, vmem_limit_bytes=48 * 1024 * 1024
        ),
        name="step",
    )(
        tokens, cotangent, weights.reshape(2 * HID, D), basis, jnp.swapaxes(master, 1, 2), first_moment, second_moment
    )
    return jnp.swapaxes(master_new, 1, 2), first_new, second_new


def solution(mesh):
    in_specs = (
        P(("dp", "hid"), None),
        P("dp", "hid"),
        P(None, "hid", None),
        P("dp", None),
        P(None, "hid", "dp"),
        P(("hid", "dp"), None, None),
        P(("hid", "dp"), None, None),
    )
    out_specs = (P(None, "hid", "dp"), P(("hid", "dp"), None, None), P(("hid", "dp"), None, None))
    return jax.shard_map(
        on_device, mesh=mesh, in_specs=in_specs, out_specs=out_specs, check_vma=False
    )
```

time: 888 us -> 96.8 us (0.11)
  waiting for transfers between devices: 851 us -> 0 us
  Pallas kernels: 0 us -> 88.7 us
  matrix products: 16.9 us -> 0 us
  between operations: 14.5 us -> 0.66 us
    unnamed x5 -> x0, waiting for transfers between devices: 527 us -> none
    all_gather x3 -> x0, waiting for transfers between devices: 324 us -> none  [the longest x1 118 us: on_device(): direction = lax.all_gather(direction_share, 'dp', axis=0, tiled=True)]
    pallas_call x0 -> x1, Pallas kernels: none -> 88.7 us  [on_device(): pl.pallas_call(kernel, out_shape=(jax.ShapeDtypeStruct((2, 64, HID), F32)...]
    dot_general x6 -> x0, matrix products: 16.9 us -> none  [the longest x1 4.94 us: on_device(): lax.dot_general(group_tokens, weights[0], contract_cols, preferred_elemen...]
  transfers between devices with their start and end apart: 4 -> 0, of which waited for: 4 -> 0; matrix products, arithmetic and copies ran while one was open for 1% -> 0% of each run, Pallas kernels for 0% -> 0%
where the time goes in v1:
time: 96.8 us; the launch traced here: 96.3 us
  Pallas kernels  88.7 us (92%)
  local copies, waits for them, and re-layouts  6.96 us (7%)
    pallas_call x1, Pallas kernels, on_device(): pl.pallas_call(kernel, out_shape=(jax.ShapeDtypeStruct((2, 64, HID), F32)...  88.7 us
    unnamed x15, local copies, waits for them, and re-layouts  6.96 us

profile of v1, /device:TPU:1, one launch (start us, length us, event | category | flops | bytes accessed | tf_op | source)
XLA Modules:
  0.0 96.3 jit_solution(13118832624546645389)
XLA Ops:
  0.6 0.0 copy-start
  0.6 1.0 %copy-done = f32[2,640,64]{1,2,0:T(8,128)S(1)} copy-done((f32[2,640,64]{1,2,0:T(8,128)S(1)}, f32[2,640,64]{1,2,0:T(8,128)}, u32[]{:S(2)}) %copy-start) | copy-done | bytes 327704
  1.6 0.0 copy-start.1
  1.6 0.9 copy-done.1
  2.6 0.0 copy-start.2
  2.6 0.9 copy-done.2
  3.5 0.0 copy-start.3
  3.5 0.8 copy-done.3
  4.2 0.0 copy-start.4
  4.2 0.7 copy-done.4
  4.9 0.0 copy-start.5
  4.9 0.7 copy-done.5
  5.7 88.7 %step.1 = (f32[2,64,640]{2,1,0:T(8,128)S(1)}, f32[10,2,256]{2,1,0:T(2,128)S(1)}, f32[10,2,256]{2,1,0:T(2,128)S(1)}) custom-call(bf16[16,4096]{1,0:T(8,128)(2,1)S(1)} %copy-done.2, bf16[192,640]{1,0:T(8,128)(2,1)S(1)} %copy-done.1, bf16[1280,4096]{1,0:T(8,128)(2,1)} %bitcast.5, bf16[64,256]{1,0:T(8,128)(2,1)S(1)} %copy-done.3, f32[2,64,640]{2,1,0:T(8,128)S(1)} %bitcast.3, ...), custom_call_target="tpu_custom_call" | custom-call | tf_op jit(solution)/shard_map/step/pallas_call | solution.py:465
  94.4 0.7 copy.13
  95.1 0.6 copy.14
  95.7 0.6 copy.15
Async XLA Ops:
  0.6 1.0 %copy-start = (f32[2,640,64]{1,2,0:T(8,128)S(1)}, f32[2,640,64]{1,2,0:T(8,128)}, u32[]{:S(2)}) copy-start(f32[2,640,64]{1,2,0:T(8,128)} %param.11) | copy-start | bytes 983044
  1.6 0.9 copy-start.1
  2.6 0.9 copy-start.2
  3.5 0.8 copy-start.3
  4.2 0.7 copy-start.4
  4.9 0.7 copy-start.5

commit v2 on v1

v2 whole, which is shorter than its diff:
```python
import functools

import jax
import jax.numpy as jnp
from jax import lax
from jax.experimental import pallas as pl
from jax.experimental.pallas import tpu as pltpu
from jax.sharding import PartitionSpec as P

MESH = pl.DeviceIdType.MESH
F32 = jnp.float32
BF16 = jnp.bfloat16

beta_first = 0.9
beta_second = 0.95
step_size = 0.05
adam_epsilon = 1e-08

NX, NY, NL, NH = 4, 8, 4, 3
D, HID, RANK, TOK = 4096, 640, 256, 16
GROUP = 192
CHUNKS = 4
CW = D // CHUNKS
HALF = RANK // 2
SHARE = 10
BLOCK = 4 * SHARE
NB = NY * NL


def dot_nt(a, b):
    return lax.dot_general(a, b, (((1,), (1,)), ((), ())), preferred_element_type=F32)


def dot_nn(a, b):
    return lax.dot_general(a, b, (((1,), (0,)), ((), ())), preferred_element_type=F32)


def split(a):
    hi = a.astype(BF16)
    return hi, (a - hi.astype(F32)).astype(BF16)


def kernel(
    tok_in, cot_in, w_in, bas_in, mas_in, fm_in, sm_in,
    mas_out, fn_out, sn_out,
    tok, w, bas, cot, mas, fm, sm, fmx, smx, fmb, smb,
    cot_t, pre, grad, halves, swap, total, part_a, part_b, mid_a, mid_b, last_a, last_b,
    dirs, dirs_w, fn_b, sn_b, fn_x, sn_x,
    local_sem, z_send, z_recv, x_send, x_recv, xx_send, xx_recv, xd_send, xd_recv,
    bz_send, bz_recv, ya_send, ya_recv, yb_send, yb_recv, bc_send, bc_recv,
    m_send, m_recv, s_send, s_recv, r1_send, r1_recv, r2_send, r2_recv,
    g1_send, g1_recv, ga_send, ga_recv, gb_send, gb_recv, gc_send, gc_recv, o_send, o_recv,
):
    dp, hid = lax.axis_index("dp"), lax.axis_index("hid")
    core = lax.rem(dp, 2)
    y = lax.rem(lax.div(dp, 2), NY)
    zl = lax.div(dp, 2 * NY)
    x = lax.rem(hid, NX)
    zh = lax.div(hid, NX)

    def at(core_=core, y_=y, zl_=zl, x_=x, zh_=zh):
        return {"dp": (zl_ * NY + y_) * 2 + core_, "hid": zh_ * NX + x_}

    def turn(v, by, n):
        return lax.rem(v + (by + n), n)

    x_up, x_down, x_far = turn(x, 1, NX), turn(x, -1, NX), turn(x, 2, NX)
    mate = at(core_=1 - core)

    peers = [at(x_=x_up), at(x_=x_down), at(x_=x_far), mate]
    peers += [at(zh_=turn(zh, o, NH)) for o in range(1, NH)]
    peers += [at(zl_=turn(zl, o, NL)) for o in range(1, NL)]
    peers += [at(y_=turn(y, o, NY)) for o in range(1, NY)]

    loads = [
        pltpu.make_async_copy(tok_in, tok.at[pl.ds(pl.multiple_of(hid * TOK, TOK), TOK)], local_sem.at[0]),
        pltpu.make_async_copy(bas_in, bas.at[0, y, core], local_sem.at[1]),
        pltpu.make_async_copy(fm_in, fm, local_sem.at[2]),
        pltpu.make_async_copy(sm_in, sm, local_sem.at[3]),
        pltpu.make_async_copy(cot_in, cot, local_sem.at[4]),
        pltpu.make_async_copy(w_in, w, local_sem.at[5]),
        pltpu.make_async_copy(mas_in, mas, local_sem.at[6]),
    ]
    for load in loads:
        load.start()

    barrier = pltpu.get_barrier_semaphore()
    for peer in peers:
        pl.semaphore_signal(barrier, inc=1, device_id=peer, device_id_type=MESH)
    pl.semaphore_wait(barrier, len(peers))

    sends = []

    def remote(src, dst, send, recv, to):
        return pltpu.make_async_remote_copy(
            src_ref=src, dst_ref=dst, send_sem=send, recv_sem=recv, device_id=to, device_id_type=MESH
        )

    def push(*args):
        copy = remote(*args)
        copy.start()
        sends.append(copy)

    def rows_of(zh_, x_):
        return pl.ds(pl.multiple_of((zh_ * NX + x_) * TOK, TOK), TOK)

    def columns(k, half=None):
        if half is None:
            return pl.ds(k * CW, CW)
        return pl.ds(k * CW + half * (CW // 2), CW // 2)

    own_rows = rows_of(zh, x)

    def send_z(k):
        for o in (1, 2):
            push(tok_in.at[:, columns(k)], tok.at[own_rows, columns(k)], z_send.at[o - 1, k], z_recv.at[o - 1, k],
                 at(zh_=turn(zh, o, NH)))

    def wait_z(k):
        for o in (1, 2):
            spot = tok.at[rows_of(turn(zh, -o, NH), x), columns(k)]
            remote(spot, spot, z_send.at[o - 1, k], z_recv.at[o - 1, k], at(zh_=turn(zh, -o, NH))).wait_recv()

    def send_x(h, k):
        rows = rows_of(turn(zh, -h, NH), x)
        src = tok_in.at[:, columns(k)] if h == 0 else tok.at[rows, columns(k)]
        for d, to in enumerate((x_up, x_down)):
            push(src, tok.at[rows, columns(k)], x_send.at[h, d, k], x_recv.at[h, d, k], at(x_=to))

    def pass_x(h, k):
        source = turn(zh, -h, NH)
        for d, (came, to) in enumerate(((x_down, x_up), (x_up, x_down))):
            spot = tok.at[rows_of(source, came), columns(k)]
            remote(spot, spot, x_send.at[h, d, k], x_recv.at[h, d, k], at(x_=came)).wait_recv()
            piece = tok.at[rows_of(source, came), columns(k, d)]
            push(piece, piece, xx_send.at[h, d, k], xx_recv.at[h, d, k], at(x_=to))

    def send_far(h):
        spot = tok.at[rows_of(turn(zh, -h, NH), x), columns(CHUNKS - 1)]
        push(spot, spot, xd_send.at[h - 1], xd_recv.at[h - 1], at(x_=x_far))

    def wait_x(h, k):
        for d, came in enumerate((x_down, x_up)):
            spot = tok.at[rows_of(turn(zh, -h, NH), came), columns(k)]
            remote(spot, spot, x_send.at[h, d, k], x_recv.at[h, d, k], at(x_=came)).wait_recv()

    def wait_xx(k):
        for h in range(NH):
            rows = rows_of(turn(zh, -h, NH), x_far)
            if h > 0 and k == CHUNKS - 1:
                spot = tok.at[rows, columns(k)]
                remote(spot, spot, xd_send.at[h - 1], xd_recv.at[h - 1], at(x_=x_far)).wait_recv()
                continue
            for d in range(2):
                piece = tok.at[rows, columns(k, d)]
                remote(piece, piece, xx_send.at[h, d, k], xx_recv.at[h, d, k], at(x_=x_up)).wait_recv()

    def shards(part, by, half=None, core_=core):
        spot = (0 if part == 0 else pl.ds(1, NL - 1), turn(y, by, NY), core_)
        return bas.at[spot if half is None else spot + (pl.ds(32 * half, 32),)]

    steps = (1, -1, 2, -2)
    later = ((-3, None), (-4, 0), (3, None), (4, 1))

    def send_bz():
        for o in range(1, NL):
            push(bas_in, bas.at[o, y, core], bz_send.at[o - 1], bz_recv.at[o - 1], at(zl_=turn(zl, o, NL)))

    def wait_bz():
        for o in range(1, NL):
            spot = bas.at[o, y, core]
            remote(spot, spot, bz_send.at[o - 1], bz_recv.at[o - 1], at(zl_=turn(zl, -o, NL))).wait_recv()

    def send_ya(part):
        for i, step in enumerate(steps):
            src = bas_in if part == 0 else shards(1, 0)
            push(src, shards(part, 0), ya_send.at[part, i], ya_recv.at[part, i], at(y_=turn(y, step, NY)))

    def pass_y(part):
        for i in (2, 3, 0, 1):
            spot = shards(part, -steps[i])
            remote(spot, spot, ya_send.at[part, i], ya_recv.at[part, i], at(y_=turn(y, -steps[i], NY))).wait_recv()
            if i >= 2:
                sign, d = (1, 0) if i == 2 else (-1, 1)
                push(spot, spot, yb_send.at[part, 2 * d], yb_recv.at[part, 2 * d], at(y_=turn(y, sign, NY)))
                piece = shards(part, -steps[i], d)
                push(piece, piece, yb_send.at[part, 2 * d + 1], yb_recv.at[part, 2 * d + 1], at(y_=turn(y, 2 * sign, NY)))

    def wait_yb(part):
        for i, (by, half) in enumerate(later):
            spot = shards(part, by, half)
            remote(spot, spot, yb_send.at[part, i], yb_recv.at[part, i], at(y_=turn(y, 1, NY))).wait_recv()

    def send_bc(by):
        spot = bas.at[:, turn(y, by, NY), core]
        push(spot, spot, bc_send.at[by % NY], bc_recv.at[by % NY], mate)

    def wait_bc():
        for by in range(NY):
            spot = bas.at[:, turn(y, by, NY), 1 - core]
            remote(spot, spot, bc_send.at[by], bc_recv.at[by], mate).wait_recv()

    def products(k):
        def body(i, carry):
            rows = pl.ds(pl.multiple_of(i * HID, HID), HID)
            term = dot_nt(w[rows, columns(k)], tok[:, columns(k)])
            if k == 0:
                pre[rows, :] = term
            else:
                pre[rows, :] += term
            return carry

        lax.fori_loop(0, 2, body, 0)

    send_bz()
    send_z(0)
    send_ya(0)
    for k in range(CHUNKS):
        send_x(0, k)
    send_z(1)
    push(fm_in, fmx, m_send.at[0], m_recv.at[0], mate)
    push(sm_in, smx, m_send.at[1], m_recv.at[1], mate)
    loads[1].wait()
    loads[4].wait()
    wait_bz()
    send_ya(1)
    send_bc(0)
    cot_t[...] = cot[...].astype(F32).T

    wait_z(0)
    send_z(2)
    send_x(1, 0)
    send_x(2, 0)
    pass_x(0, 0)
    pass_x(0, 1)
    pass_y(0)
    wait_z(1)
    send_z(3)
    send_x(1, 1)
    send_x(2, 1)
    pass_x(0, 2)
    pass_x(0, 3)
    pass_x(1, 0)
    pass_x(2, 0)
    wait_z(2)
    send_x(1, 2)
    send_x(2, 2)
    pass_y(1)
    for by in (1, -1, 2, -2):
        send_bc(by)
    pass_x(1, 1)
    pass_x(2, 1)
    wait_z(3)
    send_x(1, 3)
    send_x(2, 3)
    send_far(1)
    send_far(2)
    pass_x(1, 2)
    pass_x(2, 2)
    loads[0].wait()
    loads[5].wait()
    wait_xx(0)
    products(0)
    wait_yb(0)
    wait_yb(1)
    for by in (3, -3, 4):
        send_bc(by)
    wait_xx(1)
    products(1)

    loads[2].wait()
    loads[3].wait()
    for i, spot in enumerate((fmx, smx)):
        remote(spot, spot, m_send.at[i], m_recv.at[i], mate).wait_recv()
    first = core == 0
    for own, other, block in ((fm, fmx, fmb), (sm, smx, smb)):
        for g in range(2):
            mine, theirs = own[:, g, :], other[:, g, :]
            low = jnp.where(first, mine, theirs)
            high = jnp.where(first, theirs, mine)
            base = g * 2 * SHARE
            block[pl.ds(base, SHARE), :] = jnp.where(first, low[:, :HALF], low[:, HALF:])
            block[pl.ds(base + SHARE, SHARE), :] = jnp.where(first, high[:, :HALF], high[:, HALF:])

    wait_xx(2)
    products(2)
    wait_bc()
    wait_x(1, 3)
    wait_x(2, 3)
    wait_xx(3)
    products(3)

    projected = None
    for o in range(NL):
        slab = pl.ds(pl.multiple_of(turn(zl, -o, NL) * (D // NL), D // NL), D // NL)
        term = dot_nn(tok[:, slab], bas[o].reshape(D // NL, RANK))
        projected = term if o == 0 else projected + term
    proj_hi, proj_lo = split(projected)

    PART = HID // 2

    def to_blocks(m, carry):
        rows = pl.ds(pl.multiple_of(m * BLOCK, BLOCK), BLOCK)
        gate, up = grad[0, rows, :], grad[1, rows, :]
        n = 2 * SHARE
        for j in range(2):
            for h in range(2):
                lanes = slice(h * HALF, (h + 1) * HALF)
                halves[h, 2 * m + j, pl.ds(0, n), :] = gate[j * n:(j + 1) * n, lanes]
                halves[h, 2 * m + j, pl.ds(n, n), :] = up[j * n:(j + 1) * n, lanes]
        return carry

    def swap_part(i):
        part = pl.ds(i * (NB // 2), NB // 2)
        return halves.at[1 - core, part], swap.at[part], s_send.at[i], s_recv.at[i], mate

    for i in range(2):
        rows, up_rows = pl.ds(i * PART, PART), pl.ds(HID + i * PART, PART)
        pre_gate, pre_up, upstream = pre[rows, :], pre[up_rows, :], cot_t[rows, :]
        s = jax.nn.sigmoid(pre_gate)
        grad_gate = upstream * pre_up * (s * (1.0 + pre_gate * (1.0 - s)))
        grad_up = upstream * (pre_gate * s)
        for g, value in enumerate((grad_gate, grad_up)):
            hi, lo = split(value)
            grad[g, rows, :] = dot_nn(hi, proj_hi) + dot_nn(lo, proj_hi) + dot_nn(hi, proj_lo)
        lax.fori_loop(i * (NB // 4), (i + 1) * (NB // 4), to_blocks, 0)
        push(*swap_part(i))

    def add_part(i):
        remote(*swap_part(i)).wait_recv()

        def add_swap(b, carry):
            total[lax.div(b, NY), lax.rem(b, NY)] = halves[core, b] + swap[b]
            return carry

        lax.fori_loop(i * (NB // 2), (i + 1) * (NB // 2), add_swap, 0)

    def adam(g):
        first_new = beta_first * fmb[...] + (1.0 - beta_first) * g
        second_new = beta_second * smb[...] + (1.0 - beta_second) * g * g
        fn_b[...] = first_new
        sn_b[...] = second_new
        return first_new / (jnp.sqrt(second_new) + adam_epsilon)

    def swap_outputs():
        for i, (src, dst) in enumerate(((fn_b, fn_x), (sn_b, sn_x))):
            remote(src, dst, o_send.at[i], o_recv.at[i], mate).start()

    @pl.when(core == 0)
    def _():
        copies = []

        def go(*args):
            copy = remote(*args)
            copy.start()
            copies.append(copy)

        def came(spot, send, recv):
            remote(spot, spot, send, recv, mate).wait_recv()

        for i in range(2):
            add_part(i)
            part = pl.ds(i * (NL // 2), NL // 2)
            for o in range(1, NY):
                go(total.at[part, turn(y, o, NY)], part_a.at[o - 1, part], r1_send.at[i, o - 1], r1_recv.at[i, o - 1],
                   at(y_=turn(y, o, NY)))
        for i in range(2):
            part = pl.ds(i * (NL // 2), NL // 2)
            value = total[part, y]
            for o in range(1, NY):
                came(part_a.at[o - 1, part], r1_send.at[i, o - 1], r1_recv.at[i, o - 1])
                value += part_a[o - 1, part]
            mid_a[part] = value
        for o in range(1, NL):
            go(mid_a.at[turn(zl, o, NL)], last_a.at[o - 1], r2_send.at[o - 1], r2_recv.at[o - 1], at(zl_=turn(zl, o, NL)))
        value = mid_a[zl]
        for o in range(1, NL):
            came(last_a.at[o - 1], r2_send.at[o - 1], r2_recv.at[o - 1])
            value += last_a[o - 1]
        own, rest = dirs.at[0, 0, y], dirs.at[0, pl.ds(1, NL - 1), y]
        dirs[0, 0, y] = adam(value)
        for o in range(1, NL):
            go(own, dirs.at[0, o, y], g1_send.at[o - 1], g1_recv.at[o - 1], at(zl_=turn(zl, o, NL)))
        for o in range(1, NY):
            go(own, own, ga_send.at[o - 1], ga_recv.at[o - 1], at(y_=turn(y, o, NY)))
        swap_outputs()
        for o in range(1, NL):
            came(dirs.at[0, o, y], g1_send.at[o - 1], g1_recv.at[o - 1])
        for o in range(1, NY):
            go(rest, rest, gb_send.at[o - 1], gb_recv.at[o - 1], at(y_=turn(y, o, NY)))
        go(dirs.at[0, :, y], dirs.at[0, :, y], gc_send.at[0], gc_recv.at[0], mate)
        for o in range(1, NY):
            source = turn(y, -o, NY)
            came(dirs.at[0, 0, source], ga_send.at[o - 1], ga_recv.at[o - 1])
            came(dirs.at[0, pl.ds(1, NL - 1), source], gb_send.at[o - 1], gb_recv.at[o - 1])
            go(dirs.at[0, :, source], dirs.at[0, :, source], gc_send.at[o], gc_recv.at[o], mate)
        for o in range(NL):
            came(dirs.at[1, turn(zl, -o, NL)], gc_send.at[NY + o], gc_recv.at[NY + o])
        for copy in copies:
            copy.wait_send()

    @pl.when(core == 1)
    def _():
        copies = []

        def go(*args):
            copy = remote(*args)
            copy.start()
            copies.append(copy)

        def came(spot, send, recv):
            remote(spot, spot, send, recv, mate).wait_recv()

        firsts = []
        for o in range(1, NL):
            to = turn(zl, o, NL)
            firsts.append((to, remote(total.at[to], part_b.at[o - 1], r1_send.at[0, o - 1], r1_recv.at[0, o - 1], at(zl_=to))))
        for i in range(2):
            add_part(i)
            for to, copy in firsts:
                pl.when(lax.div(to, NL // 2) == i)(copy.start)
        value = total[zl]
        for o in range(1, NL):
            came(part_b.at[o - 1], r1_send.at[0, o - 1], r1_recv.at[0, o - 1])
            value += part_b[o - 1]
        mid_b[...] = value
        for o in range(1, NY):
            go(mid_b.at[turn(y, o, NY)], last_b.at[o - 1], r2_send.at[o - 1], r2_recv.at[o - 1], at(y_=turn(y, o, NY)))
        value = mid_b[y]
        for o in range(1, NY):
            came(last_b.at[o - 1], r2_send.at[o - 1], r2_recv.at[o - 1])
            value += last_b[o - 1]
        own, rest = dirs.at[1, zl, 0], dirs.at[1, zl, pl.ds(1, NY - 1)]
        dirs[1, zl, 0] = adam(value)
        for o in range(1, NY):
            go(own, dirs.at[1, zl, o], g1_send.at[o - 1], g1_recv.at[o - 1], at(y_=turn(y, o, NY)))
        for o in range(1, NL):
            go(own, own, ga_send.at[o - 1], ga_recv.at[o - 1], at(zl_=turn(zl, o, NL)))
        swap_outputs()
        for o in range(1, NY):
            came(dirs.at[1, zl, o], g1_send.at[o - 1], g1_recv.at[o - 1])
        for o in range(1, NL):
            go(rest, rest, gb_send.at[o - 1], gb_recv.at[o - 1], at(zl_=turn(zl, o, NL)))
        go(dirs.at[1, zl], dirs.at[1, zl], gc_send.at[NY], gc_recv.at[NY], mate)
        for o in range(1, NL):
            source = turn(zl, -o, NL)
            came(dirs.at[1, source, 0], ga_send.at[o - 1], ga_recv.at[o - 1])
            came(dirs.at[1, source, pl.ds(1, NY - 1)], gb_send.at[o - 1], gb_recv.at[o - 1])
            go(dirs.at[1, source], dirs.at[1, source], gc_send.at[NY + o], gc_recv.at[NY + o], mate)
        for o in range(NY):
            source = turn(y, -o, NY)
            came(dirs.at[0, :, source], gc_send.at[o], gc_recv.at[o])
        for to, copy in firsts:
            copy.wait_send()
        for copy in copies:
            copy.wait_send()

    for i, (own, other, out) in enumerate(((fn_b, fn_x, fn_out), (sn_b, sn_x, sn_out))):
        copy = remote(own, other, o_send.at[i], o_recv.at[i], mate)
        copy.wait_recv()
        for g in range(2):
            base = g * 2 * SHARE
            mine = jnp.where(first, own[pl.ds(base, SHARE), :], own[pl.ds(base + SHARE, SHARE), :])
            theirs = jnp.where(first, other[pl.ds(base, SHARE), :], other[pl.ds(base + SHARE, SHARE), :])
            out[:, g, pl.ds(0, HALF)] = jnp.where(first, mine, theirs)
            out[:, g, pl.ds(HALF, HALF)] = jnp.where(first, theirs, mine)
        copy.wait_send()

    def from_blocks(m, carry):
        rows = pl.ds(pl.multiple_of(m * BLOCK, BLOCK), BLOCK)
        n = 2 * SHARE
        for h in range(2):
            lanes = pl.ds(h * HALF, HALF)
            z_, y_ = lax.div(m, NY // 2), 2 * lax.rem(m, NY // 2)
            if h == 0:
                back = lax.rem(zl - z_ + NL, NL)
                even, odd = dirs[0, back, y_], dirs[0, back, y_ + 1]
            else:
                even = dirs[1, z_, lax.rem(y - y_ + NY, NY)]
                odd = dirs[1, z_, lax.rem(y - y_ - 1 + NY, NY)]
            dirs_w[0, rows, lanes] = jnp.concatenate([even[:n], odd[:n]], axis=0)
            dirs_w[1, rows, lanes] = jnp.concatenate([even[n:], odd[n:]], axis=0)
        return carry

    lax.fori_loop(0, NB // 2, from_blocks, 0)

    loads[6].wait()
    basis_own = bas[0, y, core]
    for g in range(2):
        hi, lo = split(dirs_w[g])
        lifted = dot_nt(basis_own, hi) + dot_nt(basis_own, lo)
        mas_out[g] = mas[g] - step_size * lifted

    for copy in sends:
        copy.wait_send()


def on_device(tokens, cotangent, weights, basis, master, first_moment, second_moment):
    dma, vmem = pltpu.SemaphoreType.DMA, pltpu.VMEM
    share = (SHARE, 2, RANK)
    scratch = [
        vmem((GROUP, D), BF16), vmem((2 * HID, D), BF16), vmem((NL, NY, 2, 64, RANK), BF16), vmem((GROUP, HID), BF16),
        vmem((2, 64, HID), F32), vmem(share, F32), vmem(share, F32), vmem(share, F32), vmem(share, F32),
        vmem((BLOCK, HALF), F32), vmem((BLOCK, HALF), F32),
        vmem((HID, GROUP), F32), vmem((2 * HID, GROUP), F32), vmem((2, HID, RANK), F32),
        vmem((2, NB, BLOCK, HALF), F32), vmem((NB, BLOCK, HALF), F32), vmem((NL, NY, BLOCK, HALF), F32),
        vmem((NY - 1, NL, BLOCK, HALF), F32), vmem((NL - 1, NY, BLOCK, HALF), F32),
        vmem((NL, BLOCK, HALF), F32), vmem((NY, BLOCK, HALF), F32),
        vmem((NL - 1, BLOCK, HALF), F32), vmem((NY - 1, BLOCK, HALF), F32),
        vmem((2, NL, NY, BLOCK, HALF), F32), vmem((2, HID, RANK), F32),
        vmem((BLOCK, HALF), F32), vmem((BLOCK, HALF), F32), vmem((BLOCK, HALF), F32), vmem((BLOCK, HALF), F32),
        dma((7,)),
    ]
    for shape in (
        (2, CHUNKS), (NH, 2, CHUNKS), (NH, 2, CHUNKS), (2,), (NL - 1,), (2, 4), (2, 4), (NY,),
        (2,), (2,), (2, NY - 1), (NY - 1,), (NY - 1,), (NY - 1,), (NY - 1,), (NY + NL,), (2,),
    ):
        scratch += [dma if shape is None else dma(shape)] * 2
    any_space = pl.BlockSpec(memory_space=pl.ANY)
    in_vmem = pl.BlockSpec(memory_space=pltpu.VMEM)
    master_new, first_new, second_new = pl.pallas_call(
        kernel,
        out_shape=(
            jax.ShapeDtypeStruct((2, 64, HID), F32),
            jax.ShapeDtypeStruct(share, F32),
            jax.ShapeDtypeStruct(share, F32),
        ),
        in_specs=[any_space] * 7,
        out_specs=(in_vmem,) * 3,
        scratch_shapes=scratch,
        compiler_params=pltpu.CompilerParams(
            collective_id=0, has_side_effects=True, vmem_limit_bytes=63 * 1024 * 1024
        ),
        name="step",
    )(
        tokens, cotangent, weights.reshape(2 * HID, D), basis, jnp.swapaxes(master, 1, 2), first_moment, second_moment
    )
    return jnp.swapaxes(master_new, 1, 2), first_new, second_new


def solution(mesh):
    in_specs = (
        P(("dp", "hid"), None),
        P("dp", "hid"),
        P(None, "hid", None),
        P("dp", None),
        P(None, "hid", "dp"),
        P(("hid", "dp"), None, None),
        P(("hid", "dp"), None, None),
    )
    out_specs = (P(None, "hid", "dp"), P(("hid", "dp"), None, None), P(("hid", "dp"), None, None))
    return jax.shard_map(
        on_device, mesh=mesh, in_specs=in_specs, out_specs=out_specs, check_vma=False
    )
```

time: 96.8 us -> 87.1 us (0.90)
  Pallas kernels: 88.7 us -> 81.8 us
  local copies, waits for them, and re-layouts: 6.96 us -> 4.39 us
    pallas_call x1, Pallas kernels: 88.7 us -> 81.8 us  [on_device(): pl.pallas_call(kernel, out_shape=(jax.ShapeDtypeStruct((2, 64, HID), F32)...]
    unnamed x15 -> x3, local copies, waits for them, and re-layouts: 6.96 us -> 4.39 us
where the time goes in v2:
time: 87.1 us; the launch traced here: 86.8 us
  Pallas kernels  81.8 us (94%)
  local copies, waits for them, and re-layouts  4.39 us (5%)
    pallas_call x1, Pallas kernels, on_device(): pl.pallas_call(kernel, out_shape=(jax.ShapeDtypeStruct((2, 64, HID), F32)...  81.8 us
    unnamed x3, local copies, waits for them, and re-layouts  4.39 us

profile of v2, /device:TPU:1, one launch (start us, length us, event | category | flops | bytes accessed | tf_op | source)
XLA Modules:
  0.0 86.8 jit_solution(8328222590037955770)
XLA Ops:
  0.6 81.8 %step.1 = (f32[2,64,640]{2,1,0:T(8,128)}, f32[10,2,256]{2,1,0:T(2,128)}, f32[10,2,256]{2,1,0:T(2,128)}) custom-call(bf16[16,4096]{1,0:T(8,128)(2,1)} %tok_in.1, bf16[192,640]{1,0:T(8,128)(2,1)} %cot_in.1, bf16[1280,4096]{1,0:T(8,128)(2,1)} %bitcast.3, bf16[64,256]{1,0:T(8,128)(2,1)} %bas_in.1, f32[2,64,640]{2,1,0:T(8,128)} %bitcast.4, f32[10,2,256]{2,1,0:T(2,128)} %fm_in.1, ...), custom_call_target="tpu_custom_call" | custom-call | tf_op jit(solution)/shard_map/step/pallas_call | solution.py:521
  82.4 1.7 %copy.13 = f32[2,640,64]{1,2,0:T(8,128)} copy(f32[2,640,64]{1,2,0:T(8,128)} %bitcast.5) | data formatting | bytes 655360
  84.1 1.3 %copy.14 = f32[10,2,256]{2,1,0:T(2,128)} copy(f32[10,2,256]{2,1,0:T(2,128)} %get-tuple-element.13) | data formatting | bytes 40960
  85.5 1.3 %copy.15 = f32[10,2,256]{2,1,0:T(2,128)} copy(f32[10,2,256]{2,1,0:T(2,128)} %get-tuple-element.14) | data formatting | bytes 40960

commit v3 on v2

--- a/solution.py
+++ b/solution.py
@@ -25,6 +25,7 @@
 SHARE = 10
 BLOCK = 4 * SHARE
 NB = NY * NL
+CUT = 24
 
 
 def dot_nt(a, b):
@@ -44,12 +45,13 @@
     tok_in, cot_in, w_in, bas_in, mas_in, fm_in, sm_in,
     mas_out, fn_out, sn_out,
     tok, w, bas, cot, mas, fm, sm, fmx, smx, fmb, smb,
-    cot_t, pre, grad, halves, swap, total, part_a, part_b, mid_a, mid_b, last_a, last_b,
-    dirs, dirs_w, fn_b, sn_b, fn_x, sn_x,
+    cot_t, pre, grad, halves, swap, total_y, total_z, part_y, part_z, mid_y, mid_z, last_y, last_z,
+    dirs_y, dirs_z, dirs_w, fn_b, sn_b, fn_x, sn_x,
     local_sem, z_send, z_recv, x_send, x_recv, xx_send, xx_recv, xd_send, xd_recv,
     bz_send, bz_recv, ya_send, ya_recv, yb_send, yb_recv, bc_send, bc_recv,
-    m_send, m_recv, s_send, s_recv, r1_send, r1_recv, r2_send, r2_recv,
-    g1_send, g1_recv, ga_send, ga_recv, gb_send, gb_recv, gc_send, gc_recv, o_send, o_recv,
+    m_send, m_recv, s_send, s_recv, ry_send, ry_recv, rz_send, rz_recv, ty_send, ty_recv, tz_send, tz_recv,
+    gz_send, gz_recv, gy_send, gy_recv, ga_send, ga_recv, gb_send, gb_recv, gc_send, gc_recv, gd_send, gd_recv,
+    gm_send, gm_recv, o_send, o_recv,
 ):
     dp, hid = lax.axis_index("dp"), lax.axis_index("hid")
     core = lax.rem(dp, 2)
@@ -211,6 +213,10 @@
             return carry
 
         lax.fori_loop(0, 2, body, 0)
+
+    def project(k):
+        slab = bas[turn(zl, -k, NL)].reshape(CW, RANK)
+        return dot_nn(tok[:, columns(k)], slab)
 
     send_bz()
     send_z(0)
@@ -285,17 +291,15 @@
     wait_xx(2)
     products(2)
     wait_bc()
+    projected = project(0)
+    for k in range(1, CHUNKS - 1):
+        projected += project(k)
     wait_x(1, 3)
     wait_x(2, 3)
     wait_xx(3)
     products(3)
 
-    projected = None
-    for o in range(NL):
-        slab = pl.ds(pl.multiple_of(turn(zl, -o, NL) * (D // NL), D // NL), D // NL)
-        term = dot_nn(tok[:, slab], bas[o].reshape(D // NL, RANK))
-        projected = term if o == 0 else projected + term
-    proj_hi, proj_lo = split(projected)
+    proj_hi, proj_lo = split(projected + project(CHUNKS - 1))
 
     PART = HID // 2
 
@@ -326,134 +330,94 @@
         lax.fori_loop(i * (NB // 4), (i + 1) * (NB // 4), to_blocks, 0)
         push(*swap_part(i))
 
-    def add_part(i):
+    def came(spot, send, recv):
+        remote(spot, spot, send, recv, mate).wait_recv()
+
+    ahead = []
+    for o in range(1, NL):
+        to = turn(zl, o, NL)
+        ahead.append((to, remote(total_z.at[to], part_z.at[o - 1], rz_send.at[o - 1], rz_recv.at[o - 1], at(zl_=to))))
+        sends.append(ahead[-1][1])
+    for i in range(2):
         remote(*swap_part(i)).wait_recv()
 
         def add_swap(b, carry):
-            total[lax.div(b, NY), lax.rem(b, NY)] = halves[core, b] + swap[b]
+            value = halves[core, b] + swap[b]
+            total_y[lax.div(b, NY), lax.rem(b, NY)] = value[:CUT]
+            total_z[lax.div(b, NY), lax.rem(b, NY)] = value[CUT:]
             return carry
 
         lax.fori_loop(i * (NB // 2), (i + 1) * (NB // 2), add_swap, 0)
-
-    def adam(g):
-        first_new = beta_first * fmb[...] + (1.0 - beta_first) * g
-        second_new = beta_second * smb[...] + (1.0 - beta_second) * g * g
-        fn_b[...] = first_new
-        sn_b[...] = second_new
+        for to, copy in ahead:
+            pl.when(lax.div(to, NL // 2) == i)(copy.start)
+        part = pl.ds(i * (NL // 2), NL // 2)
+        for o in range(1, NY):
+            to = turn(y, o, NY)
+            push(total_y.at[part, to], part_y.at[o - 1, part], ry_send.at[i, o - 1], ry_recv.at[i, o - 1], at(y_=to))
+
+    for i in range(2):
+        part = pl.ds(i * (NL // 2), NL // 2)
+        value = total_y[part, y]
+        for o in range(1, NY):
+            came(part_y.at[o - 1, part], ry_send.at[i, o - 1], ry_recv.at[i, o - 1])
+            value += part_y[o - 1, part]
+        mid_y[part] = value
+    for o in range(1, NL):
+        to = turn(zl, o, NL)
+        push(mid_y.at[to], last_y.at[o - 1], tz_send.at[o - 1], tz_recv.at[o - 1], at(zl_=to))
+    value = total_z[zl]
+    for o in range(1, NL):
+        came(part_z.at[o - 1], rz_send.at[o - 1], rz_recv.at[o - 1])
+        value += part_z[o - 1]
+    mid_z[...] = value
+    for o in range(1, NY):
+        to = turn(y, o, NY)
+        push(mid_z.at[to], last_z.at[o - 1], ty_send.at[o - 1], ty_recv.at[o - 1], at(y_=to))
+
+    def adam(g, rows):
+        first_new = beta_first * fmb[rows] + (1.0 - beta_first) * g
+        second_new = beta_second * smb[rows] + (1.0 - beta_second) * g * g
+        fn_b[rows] = first_new
+        sn_b[rows] = second_new
         return first_new / (jnp.sqrt(second_new) + adam_epsilon)
 
-    def swap_outputs():
-        for i, (src, dst) in enumerate(((fn_b, fn_x), (sn_b, sn_x))):
-            remote(src, dst, o_send.at[i], o_recv.at[i], mate).start()
-
-    @pl.when(core == 0)
-    def _():
-        copies = []
-
-        def go(*args):
-            copy = remote(*args)
-            copy.start()
-            copies.append(copy)
-
-        def came(spot, send, recv):
-            remote(spot, spot, send, recv, mate).wait_recv()
-
-        for i in range(2):
-            add_part(i)
-            part = pl.ds(i * (NL // 2), NL // 2)
-            for o in range(1, NY):
-                go(total.at[part, turn(y, o, NY)], part_a.at[o - 1, part], r1_send.at[i, o - 1], r1_recv.at[i, o - 1],
-                   at(y_=turn(y, o, NY)))
-        for i in range(2):
-            part = pl.ds(i * (NL // 2), NL // 2)
-            value = total[part, y]
-            for o in range(1, NY):
-                came(part_a.at[o - 1, part], r1_send.at[i, o - 1], r1_recv.at[i, o - 1])
-                value += part_a[o - 1, part]
-            mid_a[part] = value
-        for o in range(1, NL):
-            go(mid_a.at[turn(zl, o, NL)], last_a.at[o - 1], r2_send.at[o - 1], r2_recv.at[o - 1], at(zl_=turn(zl, o, NL)))
-        value = mid_a[zl]
-        for o in range(1, NL):
-            came(last_a.at[o - 1], r2_send.at[o - 1], r2_recv.at[o - 1])
-            value += last_a[o - 1]
-        own, rest = dirs.at[0, 0, y], dirs.at[0, pl.ds(1, NL - 1), y]
-        dirs[0, 0, y] = adam(value)
-        for o in range(1, NL):
-            go(own, dirs.at[0, o, y], g1_send.at[o - 1], g1_recv.at[o - 1], at(zl_=turn(zl, o, NL)))
-        for o in range(1, NY):
-            go(own, own, ga_send.at[o - 1], ga_recv.at[o - 1], at(y_=turn(y, o, NY)))
-        swap_outputs()
-        for o in range(1, NL):
-            came(dirs.at[0, o, y], g1_send.at[o - 1], g1_recv.at[o - 1])
-        for o in range(1, NY):
-            go(rest, rest, gb_send.at[o - 1], gb_recv.at[o - 1], at(y_=turn(y, o, NY)))
-        go(dirs.at[0, :, y], dirs.at[0, :, y], gc_send.at[0], gc_recv.at[0], mate)
-        for o in range(1, NY):
-            source = turn(y, -o, NY)
-            came(dirs.at[0, 0, source], ga_send.at[o - 1], ga_recv.at[o - 1])
-            came(dirs.at[0, pl.ds(1, NL - 1), source], gb_send.at[o - 1], gb_recv.at[o - 1])
-            go(dirs.at[0, :, source], dirs.at[0, :, source], gc_send.at[o], gc_recv.at[o], mate)
-        for o in range(NL):
-            came(dirs.at[1, turn(zl, -o, NL)], gc_send.at[NY + o], gc_recv.at[NY + o])
-        for copy in copies:
-            copy.wait_send()
-
-    @pl.when(core == 1)
-    def _():
-        copies = []
-
-        def go(*args):
-            copy = remote(*args)
-            copy.start()
-            copies.append(copy)
-
-        def came(spot, send, recv):
-            remote(spot, spot, send, recv, mate).wait_recv()
-
-        firsts = []
-        for o in range(1, NL):
-            to = turn(zl, o, NL)
-            firsts.append((to, remote(total.at[to], part_b.at[o - 1], r1_send.at[0, o - 1], r1_recv.at[0, o - 1], at(zl_=to))))
-        for i in range(2):
-            add_part(i)
-            for to, copy in firsts:
-                pl.when(lax.div(to, NL // 2) == i)(copy.start)
-        value = total[zl]
-        for o in range(1, NL):
-            came(part_b.at[o - 1], r1_send.at[0, o - 1], r1_recv.at[0, o - 1])
-            value += part_b[o - 1]
-        mid_b[...] = value
-        for o in range(1, NY):
-            go(mid_b.at[turn(y, o, NY)], last_b.at[o - 1], r2_send.at[o - 1], r2_recv.at[o - 1], at(y_=turn(y, o, NY)))
-        value = mid_b[y]
-        for o in range(1, NY):
-            came(last_b.at[o - 1], r2_send.at[o - 1], r2_recv.at[o - 1])
-            value += last_b[o - 1]
-        own, rest = dirs.at[1, zl, 0], dirs.at[1, zl, pl.ds(1, NY - 1)]
-        dirs[1, zl, 0] = adam(value)
-        for o in range(1, NY):
-            go(own, dirs.at[1, zl, o], g1_send.at[o - 1], g1_recv.at[o - 1], at(y_=turn(y, o, NY)))
-        for o in range(1, NL):
-            go(own, own, ga_send.at[o - 1], ga_recv.at[o - 1], at(zl_=turn(zl, o, NL)))
-        swap_outputs()
-        for o in range(1, NY):
-            came(dirs.at[1, zl, o], g1_send.at[o - 1], g1_recv.at[o - 1])
-        for o in range(1, NL):
-            go(rest, rest, gb_send.at[o - 1], gb_recv.at[o - 1], at(zl_=turn(zl, o, NL)))
-        go(dirs.at[1, zl], dirs.at[1, zl], gc_send.at[NY], gc_recv.at[NY], mate)
-        for o in range(1, NL):
-            source = turn(zl, -o, NL)
-            came(dirs.at[1, source, 0], ga_send.at[o - 1], ga_recv.at[o - 1])
-            came(dirs.at[1, source, pl.ds(1, NY - 1)], gb_send.at[o - 1], gb_recv.at[o - 1])
-            go(dirs.at[1, source], dirs.at[1, source], gc_send.at[NY + o], gc_recv.at[NY + o], mate)
-        for o in range(NY):
-            source = turn(y, -o, NY)
-            came(dirs.at[0, :, source], gc_send.at[o], gc_recv.at[o])
-        for to, copy in firsts:
-            copy.wait_send()
-        for copy in copies:
-            copy.wait_send()
+    own_y, rest_y = dirs_y.at[core, 0, y], dirs_y.at[core, pl.ds(1, NL - 1), y]
+    own_z, rest_z = dirs_z.at[core, zl, 0], dirs_z.at[core, zl, pl.ds(1, NY - 1)]
+
+    value = mid_y[zl]
+    for o in range(1, NL):
+        came(last_y.at[o - 1], tz_send.at[o - 1], tz_recv.at[o - 1])
+        value += last_y[o - 1]
+    dirs_y[core, 0, y] = adam(value, pl.ds(0, CUT))
+    for o in range(1, NL):
+        push(own_y, dirs_y.at[core, o, y], gz_send.at[o - 1], gz_recv.at[o - 1], at(zl_=turn(zl, o, NL)))
+    for o in range(1, NY):
+        push(own_y, own_y, ga_send.at[o - 1], ga_recv.at[o - 1], at(y_=turn(y, o, NY)))
+    value = mid_z[y]
+    for o in range(1, NY):
+        came(last_z.at[o - 1], ty_send.at[o - 1], ty_recv.at[o - 1])
+        value += last_z[o - 1]
+    dirs_z[core, zl, 0] = adam(value, pl.ds(CUT, BLOCK - CUT))
+    for o in range(1, NY):
+        push(own_z, dirs_z.at[core, zl, o], gy_send.at[o - 1], gy_recv.at[o - 1], at(y_=turn(y, o, NY)))
+    for o in range(1, NL):
+        push(own_z, own_z, gb_send.at[o - 1], gb_recv.at[o - 1], at(zl_=turn(zl, o, NL)))
+    for i, (src, dst) in enumerate(((fn_b, fn_x), (sn_b, sn_x))):
+        remote(src, dst, o_send.at[i], o_recv.at[i], mate).start()
+    for o in range(1, NL):
+        came(dirs_y.at[core, o, y], gz_send.at[o - 1], gz_recv.at[o - 1])
+    for o in range(1, NY):
+        push(rest_y, rest_y, gc_send.at[o - 1], gc_recv.at[o - 1], at(y_=turn(y, o, NY)))
+    for o in range(1, NY):
+        came(dirs_z.at[core, zl, o], gy_send.at[o - 1], gy_recv.at[o - 1])
+    for o in range(1, NL):
+        push(rest_z, rest_z, gd_send.at[o - 1], gd_recv.at[o - 1], at(zl_=turn(zl, o, NL)))
+    spot = dirs_y.at[core, :, y]
+    push(spot, spot, gm_send.at[0], gm_recv.at[0], mate)
+    spot = dirs_z.at[core, zl]
+    push(spot, spot, gm_send.at[NY], gm_recv.at[NY], mate)
+
+    loads[6].wait()
 
     for i, (own, other, out) in enumerate(((fn_b, fn_x, fn_out), (sn_b, sn_x, sn_out))):
         copy = remote(own, other, o_send.at[i], o_recv.at[i], mate)
@@ -466,25 +430,39 @@
             out[:, g, pl.ds(HALF, HALF)] = jnp.where(first, theirs, mine)
         copy.wait_send()
 
+    for o in range(1, NY):
+        source = turn(y, -o, NY)
+        came(dirs_y.at[core, 0, source], ga_send.at[o - 1], ga_recv.at[o - 1])
+        came(dirs_y.at[core, pl.ds(1, NL - 1), source], gc_send.at[o - 1], gc_recv.at[o - 1])
+        spot = dirs_y.at[core, :, source]
+        push(spot, spot, gm_send.at[o], gm_recv.at[o], mate)
+    for o in range(1, NL):
+        source = turn(zl, -o, NL)
+        came(dirs_z.at[core, source, 0], gb_send.at[o - 1], gb_recv.at[o - 1])
+        came(dirs_z.at[core, source, pl.ds(1, NY - 1)], gd_send.at[o - 1], gd_recv.at[o - 1])
+        spot = dirs_z.at[core, source]
+        push(spot, spot, gm_send.at[NY + o], gm_recv.at[NY + o], mate)
+    for o in range(NY):
+        came(dirs_y.at[1 - core, :, turn(y, -o, NY)], gm_send.at[o], gm_recv.at[o])
+    for o in range(NL):
+        came(dirs_z.at[1 - core, turn(zl, -o, NL)], gm_send.at[NY + o], gm_recv.at[NY + o])
+
     def from_blocks(m, carry):
         rows = pl.ds(pl.multiple_of(m * BLOCK, BLOCK), BLOCK)
         n = 2 * SHARE
         for h in range(2):
             lanes = pl.ds(h * HALF, HALF)
             z_, y_ = lax.div(m, NY // 2), 2 * lax.rem(m, NY // 2)
-            if h == 0:
-                back = lax.rem(zl - z_ + NL, NL)
-                even, odd = dirs[0, back, y_], dirs[0, back, y_ + 1]
-            else:
-                even = dirs[1, z_, lax.rem(y - y_ + NY, NY)]
-                odd = dirs[1, z_, lax.rem(y - y_ - 1 + NY, NY)]
+            back = lax.rem(zl - z_ + NL, NL)
+            even, odd = (
+                jnp.concatenate([dirs_y[h, back, v], dirs_z[h, z_, lax.rem(y - v + NY, NY)]], axis=0) for v in (y_, y_ + 1)
+            )
             dirs_w[0, rows, lanes] = jnp.concatenate([even[:n], odd[:n]], axis=0)
             dirs_w[1, rows, lanes] = jnp.concatenate([even[n:], odd[n:]], axis=0)
         return carry
 
     lax.fori_loop(0, NB // 2, from_blocks, 0)
 
-    loads[6].wait()
     basis_own = bas[0, y, core]
     for g in range(2):
         hi, lo = split(dirs_w[g])
@@ -493,6 +471,14 @@
 
     for copy in sends:
         copy.wait_send()
+
+
+def leave(a, b, c, a_out, b_out, c_out, sem):
+    copies = [pltpu.make_async_copy(src, dst, sem.at[i]) for i, (src, dst) in enumerate(((a, a_out), (b, b_out), (c, c_out)))]
+    for copy in copies:
+        copy.start()
+    for copy in copies:
+        copy.wait()
 
 
 def on_device(tokens, cotangent, weights, basis, master, first_moment, second_moment):
@@ -503,17 +489,19 @@
         vmem((2, 64, HID), F32), vmem(share, F32), vmem(share, F32), vmem(share, F32), vmem(share, F32),
         vmem((BLOCK, HALF), F32), vmem((BLOCK, HALF), F32),
         vmem((HID, GROUP), F32), vmem((2 * HID, GROUP), F32), vmem((2, HID, RANK), F32),
-        vmem((2, NB, BLOCK, HALF), F32), vmem((NB, BLOCK, HALF), F32), vmem((NL, NY, BLOCK, HALF), F32),
-        vmem((NY - 1, NL, BLOCK, HALF), F32), vmem((NL - 1, NY, BLOCK, HALF), F32),
-        vmem((NL, BLOCK, HALF), F32), vmem((NY, BLOCK, HALF), F32),
-        vmem((NL - 1, BLOCK, HALF), F32), vmem((NY - 1, BLOCK, HALF), F32),
-        vmem((2, NL, NY, BLOCK, HALF), F32), vmem((2, HID, RANK), F32),
+        vmem((2, NB, BLOCK, HALF), F32), vmem((NB, BLOCK, HALF), F32),
+        vmem((NL, NY, CUT, HALF), F32), vmem((NL, NY, BLOCK - CUT, HALF), F32),
+        vmem((NY - 1, NL, CUT, HALF), F32), vmem((NL - 1, NY, BLOCK - CUT, HALF), F32),
+        vmem((NL, CUT, HALF), F32), vmem((NY, BLOCK - CUT, HALF), F32),
+        vmem((NL - 1, CUT, HALF), F32), vmem((NY - 1, BLOCK - CUT, HALF), F32),
+        vmem((2, NL, NY, CUT, HALF), F32), vmem((2, NL, NY, BLOCK - CUT, HALF), F32), vmem((2, HID, RANK), F32),
         vmem((BLOCK, HALF), F32), vmem((BLOCK, HALF), F32), vmem((BLOCK, HALF), F32), vmem((BLOCK, HALF), F32),
         dma((7,)),
     ]
     for shape in (
         (2, CHUNKS), (NH, 2, CHUNKS), (NH, 2, CHUNKS), (2,), (NL - 1,), (2, 4), (2, 4), (NY,),
-        (2,), (2,), (2, NY - 1), (NY - 1,), (NY - 1,), (NY - 1,), (NY - 1,), (NY + NL,), (2,),
+        (2,), (2,), (2, NY - 1), (NL - 1,), (NY - 1,), (NL - 1,),
+        (NL - 1,), (NY - 1,), (NY - 1,), (NL - 1,), (NY - 1,), (NL - 1,), (NY + NL,), (2,),
     ):
         scratch += [dma if shape is None else dma(shape)] * 2
     any_space = pl.BlockSpec(memory_space=pl.ANY)
@@ -535,6 +523,15 @@
     )(
         tokens, cotangent, weights.reshape(2 * HID, D), basis, jnp.swapaxes(master, 1, 2), first_moment, second_moment
     )
+    results = (master_new, first_new, second_new)
+    master_new, first_new, second_new = pl.pallas_call(
+        leave,
+        out_shape=tuple(jax.ShapeDtypeStruct(a.shape, a.dtype) for a in results),
+        in_specs=[any_space] * 3,
+        out_specs=(any_space,) * 3,
+        scratch_shapes=[dma((3,))],
+        name="leave",
+    )(*results)
     return jnp.swapaxes(master_new, 1, 2), first_new, second_new
 
 

time: 87.1 us -> 95.6 us (1.098)
  Pallas kernels: 81.8 us -> 94.8 us
  local copies, waits for them, and re-layouts: 4.39 us -> 0 us
    pallas_call x0 -> x1, Pallas kernels: none -> 12.3 us  [on_device(): pl.pallas_call(leave, out_shape=tuple((jax.ShapeDtypeStruct(a.shape, a.dt...]
    unnamed x3 -> x0, local copies, waits for them, and re-layouts: 4.39 us -> none
where the time goes in v3:
time: 95.6 us; the launch traced here: 95.4 us
  Pallas kernels  94.8 us (99%)
    pallas_call x1, Pallas kernels, on_device(): pl.pallas_call(kernel, out_shape=(jax.ShapeDtypeStruct((2, 64, HID), F32)...  82.5 us
    pallas_call x1, Pallas kernels, on_device(): pl.pallas_call(leave, out_shape=tuple((jax.ShapeDtypeStruct(a.shape, a.dt...  12.3 us

profile of v3, /device:TPU:1, one launch (start us, length us, event | category | flops | bytes accessed | tf_op | source)
XLA Modules:
  0.0 95.4 jit_solution(17386870412644723957)
XLA Ops:
  0.6 82.5 %step.1 = (f32[2,64,640]{2,1,0:T(8,128)}, f32[10,2,256]{2,1,0:T(2,128)}, f32[10,2,256]{2,1,0:T(2,128)}) custom-call(bf16[16,4096]{1,0:T(8,128)(2,1)} %tok_in.1, bf16[192,640]{1,0:T(8,128)(2,1)} %cot_in.1, bf16[1280,4096]{1,0:T(8,128)(2,1)} %bitcast.3, bf16[64,256]{1,0:T(8,128)(2,1)} %bas_in.1, f32[2,64,640]{2,1,0:T(8,128)} %bitcast.4, f32[10,2,256]{2,1,0:T(2,128)} %fm_in.1, ...), custom_call_target="tpu_custom_call" | custom-call | tf_op jit(solution)/shard_map/step/pallas_call | solution.py:509
  83.1 12.3 %leave.1 = (f32[2,64,640]{2,1,0:T(8,128)}, f32[10,2,256]{2,1,0:T(2,128)}, f32[10,2,256]{2,1,0:T(2,128)}) custom-call(f32[2,64,640]{2,1,0:T(8,128)} %get-tuple-element.9.a, f32[10,2,256]{2,1,0:T(2,128)} %get-tuple-element.10.b, f32[10,2,256]{2,1,0:T(2,128)} %get-tuple-element.11.c), custom_call_target="tpu_custom_call" | custom-call | tf_op jit(solution)/shard_map/leave/pallas_call | solution.py:527

commit v4 on v2

--- a/solution.py
+++ b/solution.py
@@ -211,6 +211,10 @@
             return carry
 
         lax.fori_loop(0, 2, body, 0)
+
+    def project(k):
+        slab = bas[turn(zl, -k, NL)].reshape(CW, RANK)
+        return dot_nn(tok[:, columns(k)], slab)
 
     send_bz()
     send_z(0)
@@ -261,12 +265,12 @@
     loads[5].wait()
     wait_xx(0)
     products(0)
+    wait_xx(1)
+    products(1)
     wait_yb(0)
     wait_yb(1)
     for by in (3, -3, 4):
         send_bc(by)
-    wait_xx(1)
-    products(1)
 
     loads[2].wait()
     loads[3].wait()
@@ -285,17 +289,15 @@
     wait_xx(2)
     products(2)
     wait_bc()
+    projected = project(0)
+    for k in range(1, CHUNKS - 1):
+        projected += project(k)
     wait_x(1, 3)
     wait_x(2, 3)
     wait_xx(3)
     products(3)
 
-    projected = None
-    for o in range(NL):
-        slab = pl.ds(pl.multiple_of(turn(zl, -o, NL) * (D // NL), D // NL), D // NL)
-        term = dot_nn(tok[:, slab], bas[o].reshape(D // NL, RANK))
-        projected = term if o == 0 else projected + term
-    proj_hi, proj_lo = split(projected)
+    proj_hi, proj_lo = split(projected + project(CHUNKS - 1))
 
     PART = HID // 2
 
@@ -455,7 +457,7 @@
         for copy in copies:
             copy.wait_send()
 
-    for i, (own, other, out) in enumerate(((fn_b, fn_x, fn_out), (sn_b, sn_x, sn_out))):
+    for i, (own, other, out) in enumerate(((fn_b, fn_x, fm), (sn_b, sn_x, sm))):
         copy = remote(own, other, o_send.at[i], o_recv.at[i], mate)
         copy.wait_recv()
         for g in range(2):
@@ -465,6 +467,12 @@
             out[:, g, pl.ds(0, HALF)] = jnp.where(first, mine, theirs)
             out[:, g, pl.ds(HALF, HALF)] = jnp.where(first, theirs, mine)
         copy.wait_send()
+    leaving = [
+        pltpu.make_async_copy(fm, fn_out, local_sem.at[2]),
+        pltpu.make_async_copy(sm, sn_out, local_sem.at[3]),
+    ]
+    for copy in leaving:
+        copy.start()
 
     def from_blocks(m, carry):
         rows = pl.ds(pl.multiple_of(m * BLOCK, BLOCK), BLOCK)
@@ -489,10 +497,28 @@
     for g in range(2):
         hi, lo = split(dirs_w[g])
         lifted = dot_nt(basis_own, hi) + dot_nt(basis_own, lo)
-        mas_out[g] = mas[g] - step_size * lifted
+        mas[g] = mas[g] - step_size * lifted
+        leaving.append(pltpu.make_async_copy(mas.at[g], mas_out.at[g], local_sem.at[4 + g]))
+        leaving[-1].start()
+    for copy in leaving:
+        copy.wait()
 
     for copy in sends:
         copy.wait_send()
+
+
+def leave(master, first, second, master_out, first_out, second_out, held, held_first, held_second, sem):
+    trips = [(master.at[i], held.at[i], master_out.at[i]) for i in range(2)]
+    trips += [(first, held_first, first_out), (second, held_second, second_out)]
+    ins = [pltpu.make_async_copy(src, spot, sem.at[0, i]) for i, (src, spot, _) in enumerate(trips)]
+    outs = [pltpu.make_async_copy(spot, dst, sem.at[1, i]) for i, (_, spot, dst) in enumerate(trips)]
+    for copy in ins:
+        copy.start()
+    for came, copy in zip(ins, outs):
+        came.wait()
+        copy.start()
+    for copy in outs:
+        copy.wait()
 
 
 def on_device(tokens, cotangent, weights, basis, master, first_moment, second_moment):
@@ -517,7 +543,6 @@
     ):
         scratch += [dma if shape is None else dma(shape)] * 2
     any_space = pl.BlockSpec(memory_space=pl.ANY)
-    in_vmem = pl.BlockSpec(memory_space=pltpu.VMEM)
     master_new, first_new, second_new = pl.pallas_call(
         kernel,
         out_shape=(
@@ -526,7 +551,7 @@
             jax.ShapeDtypeStruct(share, F32),
         ),
         in_specs=[any_space] * 7,
-        out_specs=(in_vmem,) * 3,
+        out_specs=(any_space,) * 3,
         scratch_shapes=scratch,
         compiler_params=pltpu.CompilerParams(
             collective_id=0, has_side_effects=True, vmem_limit_bytes=63 * 1024 * 1024
@@ -535,6 +560,15 @@
     )(
         tokens, cotangent, weights.reshape(2 * HID, D), basis, jnp.swapaxes(master, 1, 2), first_moment, second_moment
     )
+    results = (master_new, first_new, second_new)
+    master_new, first_new, second_new = pl.pallas_call(
+        leave,
+        out_shape=tuple(jax.ShapeDtypeStruct(a.shape, a.dtype) for a in results),
+        in_specs=[any_space] * 3,
+        out_specs=(any_space,) * 3,
+        scratch_shapes=[vmem(a.shape, F32) for a in results] + [dma((2, 4))],
+        name="leave",
+    )(*results)
     return jnp.swapaxes(master_new, 1, 2), first_new, second_new
 
 

time: 87.1 us -> 84.6 us (0.971)
  local copies, waits for them, and re-layouts: 4.39 us -> 0 us
  Pallas kernels: 81.8 us -> 83.8 us
    unnamed x3 -> x0, local copies, waits for them, and re-layouts: 4.39 us -> none
    pallas_call x0 -> x1, Pallas kernels: none -> 1.73 us  [on_device(): pl.pallas_call(leave, out_shape=tuple((jax.ShapeDtypeStruct(a.shape, a.dt...]
where the time goes in v4:
time: 84.6 us; the launch traced here: 84.4 us
  Pallas kernels  83.8 us (99%)
    pallas_call x1, Pallas kernels, on_device(): pl.pallas_call(kernel, out_shape=(jax.ShapeDtypeStruct((2, 64, HID), F32)...  82.1 us
    pallas_call x1, Pallas kernels, on_device(): pl.pallas_call(leave, out_shape=tuple((jax.ShapeDtypeStruct(a.shape, a.dt...  1.73 us

profile of v4, /device:TPU:1, one launch (start us, length us, event | category | flops | bytes accessed | tf_op | source)
XLA Modules:
  0.0 84.4 jit_solution(17396823393946523740)
XLA Ops:
  0.6 82.1 %step.1 = (f32[2,64,640]{2,1,0:T(8,128)}, f32[10,2,256]{2,1,0:T(2,128)}, f32[10,2,256]{2,1,0:T(2,128)}) custom-call(bf16[16,4096]{1,0:T(8,128)(2,1)} %tok_in.1, bf16[192,640]{1,0:T(8,128)(2,1)} %cot_in.1, bf16[1280,4096]{1,0:T(8,128)(2,1)} %bitcast.3, bf16[64,256]{1,0:T(8,128)(2,1)} %bas_in.1, f32[2,64,640]{2,1,0:T(8,128)} %bitcast.4, f32[10,2,256]{2,1,0:T(2,128)} %fm_in.1, ...), custom_call_target="tpu_custom_call" | custom-call | tf_op jit(solution)/shard_map/step/pallas_call | solution.py:546
  82.7 1.7 %leave.1 = (f32[2,64,640]{2,1,0:T(8,128)}, f32[10,2,256]{2,1,0:T(2,128)}, f32[10,2,256]{2,1,0:T(2,128)}) custom-call(f32[2,64,640]{2,1,0:T(8,128)} %get-tuple-element.9.master, f32[10,2,256]{2,1,0:T(2,128)} %get-tuple-element.10.first, f32[10,2,256]{2,1,0:T(2,128)} %get-tuple-element.11.second), custom_call_target="tpu_custom_call" | custom-call | tf_op jit(solution)/shard_map/leave/pallas_call | solution.py:564

commit v5 on v4

--- a/solution.py
+++ b/solution.py
@@ -25,6 +25,7 @@
 SHARE = 10
 BLOCK = 4 * SHARE
 NB = NY * NL
+AROUND = (4, 3, 5, 2, 6, 1, 7)
 
 
 def dot_nt(a, b):
@@ -81,12 +82,11 @@
         pltpu.make_async_copy(w_in, w, local_sem.at[5]),
         pltpu.make_async_copy(mas_in, mas, local_sem.at[6]),
     ]
-    for load in loads:
-        load.start()
-
     barrier = pltpu.get_barrier_semaphore()
     for peer in peers:
         pl.semaphore_signal(barrier, inc=1, device_id=peer, device_id_type=MESH)
+    for load in loads:
+        load.start()
     pl.semaphore_wait(barrier, len(peers))
 
     sends = []
@@ -216,8 +216,8 @@
         slab = bas[turn(zl, -k, NL)].reshape(CW, RANK)
         return dot_nn(tok[:, columns(k)], slab)
 
+    send_z(0)
     send_bz()
-    send_z(0)
     send_ya(0)
     for k in range(CHUNKS):
         send_x(0, k)
@@ -363,13 +363,13 @@
         for i in range(2):
             add_part(i)
             part = pl.ds(i * (NL // 2), NL // 2)
-            for o in range(1, NY):
+            for o in AROUND:
                 go(total.at[part, turn(y, o, NY)], part_a.at[o - 1, part], r1_send.at[i, o - 1], r1_recv.at[i, o - 1],
                    at(y_=turn(y, o, NY)))
         for i in range(2):
             part = pl.ds(i * (NL // 2), NL // 2)
             value = total[part, y]
-            for o in range(1, NY):
+            for o in AROUND:
                 came(part_a.at[o - 1, part], r1_send.at[i, o - 1], r1_recv.at[i, o - 1])
                 value += part_a[o - 1, part]
             mid_a[part] = value
@@ -383,21 +383,22 @@
         dirs[0, 0, y] = adam(value)
         for o in range(1, NL):
             go(own, dirs.at[0, o, y], g1_send.at[o - 1], g1_recv.at[o - 1], at(zl_=turn(zl, o, NL)))
-        for o in range(1, NY):
+        for o in AROUND:
             go(own, own, ga_send.at[o - 1], ga_recv.at[o - 1], at(y_=turn(y, o, NY)))
         swap_outputs()
         for o in range(1, NL):
             came(dirs.at[0, o, y], g1_send.at[o - 1], g1_recv.at[o - 1])
-        for o in range(1, NY):
+        for o in AROUND:
             go(rest, rest, gb_send.at[o - 1], gb_recv.at[o - 1], at(y_=turn(y, o, NY)))
         go(dirs.at[0, :, y], dirs.at[0, :, y], gc_send.at[0], gc_recv.at[0], mate)
-        for o in range(1, NY):
+        for o in AROUND:
             source = turn(y, -o, NY)
             came(dirs.at[0, 0, source], ga_send.at[o - 1], ga_recv.at[o - 1])
             came(dirs.at[0, pl.ds(1, NL - 1), source], gb_send.at[o - 1], gb_recv.at[o - 1])
             go(dirs.at[0, :, source], dirs.at[0, :, source], gc_send.at[o], gc_recv.at[o], mate)
-        for o in range(NL):
-            came(dirs.at[1, turn(zl, -o, NL)], gc_send.at[NY + o], gc_recv.at[NY + o])
+        near = zl + 1 - 2 * lax.rem(zl, 2)
+        for n, source in enumerate((zl, turn(zl, 2, NL), near, turn(near, 2, NL))):
+            came(dirs.at[1, source], gc_send.at[NY + n], gc_recv.at[NY + n])
         for copy in copies:
             copy.wait_send()
 
@@ -426,29 +427,40 @@
             came(part_b.at[o - 1], r1_send.at[0, o - 1], r1_recv.at[0, o - 1])
             value += part_b[o - 1]
         mid_b[...] = value
-        for o in range(1, NY):
+        for o in AROUND:
             go(mid_b.at[turn(y, o, NY)], last_b.at[o - 1], r2_send.at[o - 1], r2_recv.at[o - 1], at(y_=turn(y, o, NY)))
         value = mid_b[y]
-        for o in range(1, NY):
+        for o in AROUND:
             came(last_b.at[o - 1], r2_send.at[o - 1], r2_recv.at[o - 1])
             value += last_b[o - 1]
-        own, rest = dirs.at[1, zl, 0], dirs.at[1, zl, pl.ds(1, NY - 1)]
+        own = dirs.at[1, zl, 0]
         dirs[1, zl, 0] = adam(value)
-        for o in range(1, NY):
+        for o in AROUND:
             go(own, dirs.at[1, zl, o], g1_send.at[o - 1], g1_recv.at[o - 1], at(y_=turn(y, o, NY)))
         for o in range(1, NL):
             go(own, own, ga_send.at[o - 1], ga_recv.at[o - 1], at(zl_=turn(zl, o, NL)))
         swap_outputs()
-        for o in range(1, NY):
+        for o in AROUND:
             came(dirs.at[1, zl, o], g1_send.at[o - 1], g1_recv.at[o - 1])
-        for o in range(1, NL):
-            go(rest, rest, gb_send.at[o - 1], gb_recv.at[o - 1], at(zl_=turn(zl, o, NL)))
+        near = zl + 1 - 2 * lax.rem(zl, 2)
+        far, last = turn(zl, 2, NL), turn(near, 2, NL)
+        pieces = (pl.ds(1, 4), pl.ds(5, NY - 5))
+        for i, piece in enumerate(pieces):
+            spot = dirs.at[1, zl, piece]
+            go(spot, spot, gb_send.at[i], gb_recv.at[i], at(zl_=far))
+            go(spot, spot, gb_send.at[2 + i], gb_recv.at[2 + i], at(zl_=near))
         go(dirs.at[1, zl], dirs.at[1, zl], gc_send.at[NY], gc_recv.at[NY], mate)
-        for o in range(1, NL):
-            source = turn(zl, -o, NL)
-            came(dirs.at[1, source, 0], ga_send.at[o - 1], ga_recv.at[o - 1])
-            came(dirs.at[1, source, pl.ds(1, NY - 1)], gb_send.at[o - 1], gb_recv.at[o - 1])
-            go(dirs.at[1, source], dirs.at[1, source], gc_send.at[NY + o], gc_recv.at[NY + o], mate)
+        for i, piece in enumerate(pieces):
+            spot = dirs.at[1, far, piece]
+            came(spot, gb_send.at[i], gb_recv.at[i])
+            go(spot, spot, gb_send.at[4 + i], gb_recv.at[4 + i], at(zl_=near))
+        for o in range(1, NL):
+            came(dirs.at[1, turn(zl, -o, NL), 0], ga_send.at[o - 1], ga_recv.at[o - 1])
+        for n, source in enumerate((far, near, last)):
+            if n > 0:
+                for i, piece in enumerate(pieces):
+                    came(dirs.at[1, source, piece], gb_send.at[2 * n + i], gb_recv.at[2 * n + i])
+            go(dirs.at[1, source], dirs.at[1, source], gc_send.at[NY + 1 + n], gc_recv.at[NY + 1 + n], mate)
         for o in range(NY):
             source = turn(y, -o, NY)
             came(dirs.at[0, :, source], gc_send.at[o], gc_recv.at[o])

time: 84.6 us -> 83.3 us (0.985)
  Pallas kernels: 83.8 us -> 82.5 us
    pallas_call x1, Pallas kernels: 82.1 us -> 80.8 us  [on_device(): pl.pallas_call(kernel, out_shape=(jax.ShapeDtypeStruct((2, 64, HID), F32)...]
where the time goes in v5:
time: 83.3 us; the launch traced here: 83.2 us
  Pallas kernels  82.5 us (99%)
    pallas_call x1, Pallas kernels, on_device(): pl.pallas_call(kernel, out_shape=(jax.ShapeDtypeStruct((2, 64, HID), F32)...  80.8 us
    pallas_call x1, Pallas kernels, on_device(): pl.pallas_call(leave, out_shape=tuple((jax.ShapeDtypeStruct(a.shape, a.dt...  1.73 us

profile of v5, /device:TPU:1, one launch (start us, length us, event | category | flops | bytes accessed | tf_op | source)
XLA Modules:
  0.0 83.2 jit_solution(3012030793787813570)
XLA Ops:
  0.6 80.8 %step.1 = (f32[2,64,640]{2,1,0:T(8,128)}, f32[10,2,256]{2,1,0:T(2,128)}, f32[10,2,256]{2,1,0:T(2,128)}) custom-call(bf16[16,4096]{1,0:T(8,128)(2,1)} %tok_in.1, bf16[192,640]{1,0:T(8,128)(2,1)} %cot_in.1, bf16[1280,4096]{1,0:T(8,128)(2,1)} %bitcast.3, bf16[64,256]{1,0:T(8,128)(2,1)} %bas_in.1, f32[2,64,640]{2,1,0:T(8,128)} %bitcast.4, f32[10,2,256]{2,1,0:T(2,128)} %fm_in.1, ...), custom_call_target="tpu_custom_call" | custom-call | tf_op jit(solution)/shard_map/step/pallas_call | solution.py:558
  81.4 1.7 %leave.1 = (f32[2,64,640]{2,1,0:T(8,128)}, f32[10,2,256]{2,1,0:T(2,128)}, f32[10,2,256]{2,1,0:T(2,128)}) custom-call(f32[2,64,640]{2,1,0:T(8,128)} %get-tuple-element.9.master, f32[10,2,256]{2,1,0:T(2,128)} %get-tuple-element.10.first, f32[10,2,256]{2,1,0:T(2,128)} %get-tuple-element.11.second), custom_call_target="tpu_custom_call" | custom-call | tf_op jit(solution)/shard_map/leave/pallas_call | solution.py:576
